TPU v7x, 256 devices: a whole 4x4x8 slice. The times are simulated.
256 devices in a mesh: grp: 2 (over core), ctx: 32 (over y, z), hd: 4 (over x).
Axes of the slice: x: 4, y: 4, z: 8, core: 2. Of those that a mesh axis runs over, the one named last changes fastest.
Arguments:
- q_nope: bfloat16 [2, 8192, 8192], P('grp', ('ctx', 'hd')), may hold values from -6 to 6
- q_rope: bfloat16 [2, 8192, 4096], P('grp', ('ctx', 'hd')), may hold values from -256 to 256
- prompt_latent: bfloat16 [2, 8192, 512], P('grp', ('ctx', 'hd')), may hold values from -6 to 6
- prompt_rope: bfloat16 [2, 4096, 128], P('grp', ('ctx', 'hd')), may hold values from -4 to 4
- prompt_lists: int32 [2, 128, 16], P('grp'), may hold values from 0 to 127, as said below
- owner_map: int32 [2, 128, 1], P('grp'), may hold values from 0 to 31; in each aligned block of 128 rows (0 to 127, 128 to 255, ..., all dimensions but the last counted through in order) at most 8 rows name the same one
- w_uk: bfloat16 [64, 128, 512], P('hd'), may hold values from -0.5 to 0.5
- w_uv: bfloat16 [64, 512, 128], P('hd'), may hold values from -0.75 to 0.75
- dec_nope: bfloat16 [2, 64, 8192], P('grp', None, 'hd'), may hold values from -6 to 6
- dec_rope: bfloat16 [2, 64, 4096], P('grp', None, 'hd'), may hold values from -256 to 256
- store_latent: bfloat16 [2, 4, 128, 64, 512], P('grp', None, 'ctx'), may hold values from -6 to 6
- store_rope: bfloat16 [2, 4, 128, 4096], P('grp', None, 'ctx'), may hold values from -4 to 4
- lengths: int32 [2, 4], P('grp'), may hold values from 961 to 8192, as said below
- page_lists: int32 [2, 4, 16], P('grp'), may hold values from 0 to 127, as said below
Outputs:
- pre_out: bfloat16 [2, 8192, 8192], P('grp', 'ctx', 'hd')
- dec_out: bfloat16 [2, 64, 8192], P('grp', 'ctx', 'hd')
- landed_latent: bfloat16 [2, 256, 64, 512], P('grp', 'ctx')
- landed_rope: bfloat16 [2, 256, 4096], P('grp', 'ctx')
Inputs may be any that keep to these rules, and one draw needn't show every extreme that they name: `prompt_lists`: row b of a group lists 16 distinct blocks: b itself, min(b, 15) blocks before b, and later blocks for the rest. `owner_map`: each owner receives at most 8 of the pages of one group's prompt. `lengths`: some request of each group holds all 128 pages full. `page_lists`: each request lists 16 distinct pages that hold cached tokens, always including its last two such pages.
All inputs are finite; a program needn't handle non-finite values.
Results may differ from a plain program's by a relative error of at most 0.0075.
Values may be sent and summed in bfloat16 or wider, within the bound.
No kernel may reach another device: no remote copies, remote signals or barrier semaphores. Data moves between devices by JAX's collectives and lax.ppermute only.
A program may use at most 128 MiB of HBM per device.

v0:
```python
import jax
import jax.numpy as jnp
from jax import lax
from jax.sharding import PartitionSpec as P

NOPE = 128
ROPE = 64
LAT = 512
VDIM = 128
BLK = 64
TOPK = 16


def swapped(block, axis, distance):
    count = lax.axis_size(axis)
    route = []
    for low in range(count):
        high = low | 1 << distance
        if high != low and high < count:
            route += [(low, high), (high, low)]
    return lax.ppermute(block, axis, route)


def body(
    q_nope,
    q_rope,
    prompt_latent,
    prompt_rope,
    prompt_lists,
    owner_map,
    w_uk,
    w_uv,
    dec_nope,
    dec_rope,
    store_latent,
    store_rope,
    lengths,
    page_lists,
):
    score_scale = (NOPE + ROPE) ** (-0.5)
    heads_here = w_uk.shape[0]
    offsets = jnp.arange(BLK, dtype=jnp.int32)
    nope_heads, rotary_heads = (
        lax.all_to_all(q_nope, "hd", split_axis=2, concat_axis=1, tiled=True),
        lax.all_to_all(q_rope, "hd", split_axis=2, concat_axis=1, tiled=True),
    )
    tokens_here = nope_heads.shape[1]
    query_blocks = tokens_here // BLK
    all_latent, all_rotary = (
        lax.all_gather(prompt_latent, ("ctx", "hd"), axis=1, tiled=True),
        lax.all_gather(prompt_rope, ("ctx", "hd"), axis=1, tiled=True),
    )
    block_count = all_latent.shape[1] // BLK
    latent_blocks = all_latent[0].reshape(block_count, BLK, LAT)
    rotary_blocks = all_rotary[0].reshape(block_count, BLK, ROPE)
    absorbed = jnp.einsum(
        "thn,hnl->thl",
        nope_heads[0].reshape(tokens_here, heads_here, NOPE),
        w_uk,
        preferred_element_type=jnp.float32,
    ).astype(jnp.bfloat16)
    absorbed = absorbed.reshape(query_blocks, BLK, heads_here, LAT)
    query_rotary = rotary_heads[0].reshape(query_blocks, BLK, heads_here, ROPE)
    first_block = lax.axis_index("ctx") * query_blocks
    listed = lax.dynamic_slice_in_dim(prompt_lists[0], first_block, query_blocks, 0)
    key_latent = latent_blocks[listed].reshape(query_blocks, TOPK * BLK, LAT)
    key_rotary = rotary_blocks[listed].reshape(query_blocks, TOPK * BLK, ROPE)
    key_places = (listed[:, :, None] * BLK + offsets[None, None, :]).reshape(
        query_blocks, TOPK * BLK
    )
    query_places = (first_block + jnp.arange(query_blocks, dtype=jnp.int32))[
        :, None
    ] * BLK + offsets[None, :]
    allowed = key_places[:, None, None, :] <= query_places[:, :, None, None]
    scores = jnp.einsum("bthl,bkl->bthk", absorbed, key_latent, preferred_element_type=jnp.float32)
    scores = scores + jnp.einsum(
        "bthe,bke->bthk", query_rotary, key_rotary, preferred_element_type=jnp.float32
    )
    scores = scores * score_scale
    masked = jnp.where(allowed, scores, -jnp.inf)
    peak_score = jnp.max(masked, axis=-1, keepdims=True)
    weights = jnp.where(allowed, jnp.exp(masked - peak_score), 0.0)
    totals = jnp.sum(weights, axis=-1)
    mixture = jnp.einsum(
        "bthk,bkl->bthl",
        weights.astype(jnp.bfloat16),
        key_latent,
        preferred_element_type=jnp.float32,
    )
    mixture = (mixture / totals[..., None]).astype(jnp.bfloat16)
    prefill_out = jnp.einsum(
        "bthl,hlv->bthv", mixture, w_uv, preferred_element_type=jnp.float32
    ).astype(jnp.bfloat16)
    prefill_out = prefill_out.reshape(1, tokens_here, heads_here * VDIM)
    slot_count = 2 * block_count // lax.axis_size("ctx")
    owners = owner_map[0, :, 0]
    mine = (owners == lax.axis_index("ctx")).astype(jnp.int32)
    ranking = jnp.cumsum(mine) - 1
    chooser = (
        (mine[None, :] == 1)
        & (ranking[None, :] == jnp.arange(slot_count, dtype=jnp.int32)[:, None])
    ).astype(jnp.bfloat16)
    sent_latent = (
        jnp.dot(
            chooser,
            latent_blocks.reshape(block_count, BLK * LAT),
            preferred_element_type=jnp.float32,
        )
        .astype(jnp.bfloat16)
        .reshape(slot_count, BLK, LAT)
    )
    sent_rotary = jnp.dot(
        chooser, rotary_blocks.reshape(block_count, BLK * ROPE), preferred_element_type=jnp.float32
    ).astype(jnp.bfloat16)
    landed_lat, landed_rot = swapped((sent_latent, sent_rotary), "grp", 0)
    rows_total = dec_nope.shape[1]
    requests = store_latent.shape[1]
    per_device = store_latent.shape[2]
    rows_each = rows_total // requests
    dec_absorbed = jnp.einsum(
        "qhn,hnl->qhl",
        dec_nope[0].reshape(rows_total, heads_here, NOPE),
        w_uk,
        preferred_element_type=jnp.float32,
    ).astype(jnp.bfloat16)
    dec_absorbed = dec_absorbed.reshape(requests, rows_each, heads_here, LAT)
    dec_rotary = dec_rope[0].reshape(requests, rows_each, heads_here, ROPE)
    cache_latent = store_latent[0].reshape(requests, per_device * BLK, LAT)
    cache_rotary = store_rope[0].reshape(requests, per_device * BLK, ROPE)
    page_ids = lax.axis_index("ctx") * per_device + jnp.arange(per_device, dtype=jnp.int32)
    chosen = jnp.any(page_lists[0][:, None, :] == page_ids[None, :, None], axis=-1)
    cache_places = (page_ids[:, None] * BLK + offsets[None, :]).reshape(per_device * BLK)
    usable = jnp.repeat(chosen, BLK, axis=1) & (cache_places[None, :] < lengths[0][:, None])
    usable = usable[:, None, None, :]
    dec_scores = jnp.einsum(
        "rqhl,rkl->rqhk", dec_absorbed, cache_latent, preferred_element_type=jnp.float32
    )
    dec_scores = dec_scores + jnp.einsum(
        "rqhe,rke->rqhk", dec_rotary, cache_rotary, preferred_element_type=jnp.float32
    )
    dec_scores = dec_scores * score_scale
    local_peak = jnp.max(jnp.where(usable, dec_scores, -jnp.inf), axis=-1)
    row_peak = lax.pmax(local_peak, "ctx")
    dec_weights = jnp.where(usable, jnp.exp(dec_scores - row_peak[..., None]), 0.0)
    dec_totals = jnp.sum(dec_weights, axis=-1).reshape(rows_total, heads_here)
    dec_mixture = jnp.einsum(
        "rqhk,rkl->rqhl",
        dec_weights.astype(jnp.bfloat16),
        cache_latent,
        preferred_element_type=jnp.float32,
    )
    dec_mixture = dec_mixture.reshape(rows_total, heads_here, LAT)
    summed_mixture, summed_totals = lax.psum((dec_mixture, dec_totals), "ctx")
    rows_here = rows_total // lax.axis_size("ctx")
    first_row = lax.axis_index("ctx") * rows_here
    row_mixture = lax.dynamic_slice_in_dim(summed_mixture, first_row, rows_here, 0)
    row_totals = lax.dynamic_slice_in_dim(summed_totals, first_row, rows_here, 0)
    dec_latent = (row_mixture / row_totals[..., None]).astype(jnp.bfloat16)
    decode_out = jnp.einsum(
        "qhl,hlv->qhv", dec_latent, w_uv, preferred_element_type=jnp.float32
    ).astype(jnp.bfloat16)
    decode_out = decode_out.reshape(1, dec_latent.shape[0], heads_here * VDIM)
    return (prefill_out, decode_out, landed_lat[None], landed_rot[None])


def solution(mesh):
    in_specs = (
        P("grp", ("ctx", "hd"), None),
        P("grp", ("ctx", "hd"), None),
        P("grp", ("ctx", "hd"), None),
        P("grp", ("ctx", "hd"), None),
        P("grp", None, None),
        P("grp", None, None),
        P("hd", None, None),
        P("hd", None, None),
        P("grp", None, "hd"),
        P("grp", None, "hd"),
        P("grp", None, "ctx", None, None),
        P("grp", None, "ctx", None),
        P("grp", None),
        P("grp", None, None),
    )
    out_specs = (
        P("grp", "ctx", "hd"),
        P("grp", "ctx", "hd"),
        P("grp", "ctx", None, None),
        P("grp", "ctx", None),
    )
    return jax.shard_map(body, mesh=mesh, in_specs=in_specs, out_specs=out_specs, check_vma=False)
```

profile of v0, /device:TPU:1, one launch (start us, length us, event | category | flops | bytes accessed | tf_op | source)
XLA Modules:
  0.0 527.3 jit_solution(8426614722157416932)
XLA Ops:
  15.9 119.0 %pmax.7 = f32[4,16,16]{2,1,0:T(8,128)S(1)} all-reduce(f32[4,16,16]{2,1,0:T(8,128)S(1)} %get-tuple-element.9), channel_id=1, replica_groups=mesh['grp'=2,'ctx'=32,'hd'=4] {'ctx'}, use_global_device_ids=true, to_apply=%region_4.5 | all-reduce | flops 1024 | bytes 8192 | tf_op jit(solution)/shard_map/pmax | solution.py:143
  140.0 5.3 %copy.116 = bf16[1,64,4096]{1,0,2:T(2,128)(2,1)} copy(bf16[1,64,4096]{2,1,0:T(8,128)(2,1)} %param.15) | data formatting | bytes 1048576 | tf_op args[1]
  145.9 24.4 %reduce.3 = bf16[4096,64]{1,0:T(8,128)(2,1)} reduce(bf16[4096,1,64]{2,1,0:T(2,128)(2,1)} %bitcast.103, bf16[]{:T(256)} %broadcast.145), dimensions={1}, to_apply=%bitcast.80.reduce_sub_computation | reduce | bytes 1048578
  170.3 2.6 reshape.271
  172.9 4.6 all-to-all-start.1
  178.3 9.2 %copy.110 = bf16[1,64,8192]{1,0,2:T(2,128)(2,1)} copy(bf16[1,64,8192]{2,1,0:T(8,128)(2,1)} %param.14) | data formatting | bytes 2097152 | tf_op args[0]
  187.5 46.6 %reduce.2 = bf16[8192,64]{1,0:T(8,128)(2,1)} reduce(bf16[8192,1,64]{2,1,0:T(2,128)(2,1)} %bitcast.97, bf16[]{:T(256)} %broadcast.145), dimensions={1}, to_apply=%bitcast.78.reduce_sub_computation | reduce | bytes 2097154
  234.1 4.4 reshape.269
  238.9 111.1 %psum.15 = f32[64,16]{1,0:T(8,128)S(1)} all-reduce(f32[64,16]{1,0:T(8,128)S(1)} %bitcast.116), channel_id=1, replica_groups=mesh['grp'=2,'ctx'=32,'hd'=4] {'ctx'}, use_global_device_ids=true, to_apply=%region_7.8 | all-reduce | flops 1024 | bytes 8192 | tf_op jit(solution)/shard_map/psum | solution.py:153
  349.9 4.0 all-to-all-start
  354.4 3.9 reshape.272
  358.3 5.2 copy.117
  370.3 3.1 reshape.270
  373.4 8.2 %copy.111 = bf16[1,64,8192]{2,1,0:T(8,128)(2,1)S(1)} copy(bf16[1,64,8192]{1,0,2:T(2,128)(2,1)} %bitcast.98) | data formatting | bytes 2097152 | tf_op jit(solution)/shard_map/all_to_all | solution.py:44
  385.2 3.2 convolution_convert_fusion.2
  390.2 56.8 %collective-permute-start.1 = (bf16[8,4096]{1,0:T(8,128)(2,1)S(1)}, bf16[8,4096]{1,0:T(8,128)(2,1)S(1)}, u32[]{:S(2)}, u32[]{:S(2)}) collective-permute-start(bf16[8,4096]{1,0:T(8,128)(2,1)S(1)} %convolution_convert_fusion.1), channel_id=1, source_target_pairs={{0,128},{128,0},{1,129},{129,1},{2,130},{130,2},{3,131},{131,3},{4... | collective-permute-start | bytes 196616 | tf_op jit(solution)/shard_map/ppermute | solution.py:21
  447.0 2.7 reshape_squeeze.26
  450.5 2.7 fusion.24
  453.3 6.2 %gather_fusion = bf16[64,64,512]{2,1,0:T(8,128)(2,1)} fusion(bf16[128,64,512]{2,1,0:T(8,128)(2,1)} %bitcast.96, s32[1024]{0:T(1024)S(1)} %pad_clamp_fusion), kind=kCustom, calls=%fused_computation | custom fusion | bytes 8388864 | tf_op jit(solution)/shard_map/gather | solution.py:66
  459.5 13.5 %reshape_reshape_squeeze.6 = bf16[128,32768]{1,0:T(8,128)(2,1)} reshape(bf16[1,8192,512]{2,1,0:T(8,128)(2,1)} %all-gather.3.cloned.1.call-done) | data formatting | bytes 16777216 | tf_op jit(solution)/shard_map/reshape;reshape;squeeze | solution.py:106
  472.9 4.7 convolution_convert_fusion
  478.9 8.4 %fusion.5 = f32[4,64,16,1024]{3,2,1,0:T(8,128)} fusion(bf16[4,1024,512,1]{2,1,3,0:T(8,128)(2,1)S(1)} %bitcast.101, bf16[4,64,16,512]{3,1,0,2:T(8,128)(2,1)S(1)} %bitcast.99), kind=kOutput, calls=%fused_computation.12 | convolution fusion | flops 4294967296 | bytes 25165824 | tf_op jit(solution)/shard_map/bthl,bkl->bthk/dot_general | solution.py:75
  487.2 12.7 %fusion.50 = (bf16[4,64,16,1024]{3,2,1,0:T(8,128)(2,1)}, f32[4,64,16]{2,1,0:T(8,128)S(1)}) fusion(pred[4,64,1024]{2,1,0:T(8,128)(4,1)S(1)} %broadcast_compare_fusion, f32[4,64,16,1024]{3,2,1,0:T(8,128)} %fusion.5, bf16[4,1024,64,1]{2,1,3,0:T(8,128)(2,1)S(1)} %bitcast.113, bf16[4,64,16,64]{3,2,1,0:T(8,128)(2,1)S(1)} %copy-done.5), kind=kOutput, calls=%fused_computation.64 | convolution fusion | flops 566232064 | bytes 26492928 | tf_op jit(solution)/shard_map/sub | solution.py:82
  500.0 13.9 %fusion.19 = bf16[4,64,16,128]{3,1,0,2:T(8,128)(2,1)} fusion(bf16[16,512,128]{2,1,0:T(8,128)(2,1)} %param.21, f32[4,64,16]{1,0,2:T(4,128)S(1)} %copy.121, bf16[4,1024,512,1]{2,1,0,3:T(8,128)(2,1)} %bitcast.100, bf16[4,64,16,1024]{3,2,1,0:T(8,128)(2,1)} %get-tuple-element.4), kind=kOutput, calls=%fused_computation.21 | convolution fusion | flops 4836556800 | bytes 15745024 | tf_op jit(solution)/shard_map/bthl,hlv->bthv/dot_general | solution.py:91
  (84 shorter events, 34.9 us)
Async XLA Ops:
  8.0 6.5 %copy-start = (bf16[16,128,512]{2,1,0:T(8,128)(2,1)S(1)}, bf16[16,128,512]{2,1,0:T(8,128)(2,1)}, u32[]{:S(2)}) copy-start(bf16[16,128,512]{2,1,0:T(8,128)(2,1)} %param.20) | copy-start | bytes 6291460
  8.0 380.4 %all-gather.5.cloned.1.call-start = ((), (), s32[]{:S(2)}) async-start(), calls=%async_computation.3 | async-start | bytes 1056768 | tf_op jit(solution)/shard_map/all_gather | solution.py:51
  8.7 441.8 %all-reduce.2.cloned.1.call-start = ((), (), s32[]{:S(2)}) async-start(), calls=%async_computation.4 | async-start | bytes 4194304 | tf_op jit(solution)/shard_map/psum | solution.py:153
  13.3 1.6 copy-start.4
  139.3 314.0 %all-gather.3.cloned.1.call-start = ((), (), s32[]{:S(2)}) async-start(), calls=%async_computation.2 | async-start | bytes 8454144 | tf_op jit(solution)/shard_map/all_gather | solution.py:50
  140.0 37.5 %copy-start.6 = (s32[1,128,16]{1,2,0:T(8,128)S(1)}, s32[1,128,16]{1,2,0:T(8,128)}, u32[]{:S(2)}) copy-start(s32[1,128,16]{1,2,0:T(8,128)} %param.18) | copy-start | bytes 24580
  140.0 38.0 %copy-start.9 = (s32[1,128,1]{1,2,0:T(1,128)S(1)}, s32[1,128,1]{1,2,0:T(1,128)}, u32[]{:S(2)}) copy-start(s32[1,128,1]{1,2,0:T(1,128)} %param.19) | copy-start | bytes 1540
  172.9 177.1 %all-to-all-start.1 = ((bf16[4,2,32768]{2,1,0:T(2,128)(2,1)}), bf16[4,2,32768]{2,1,0:T(2,128)(2,1)}, u32[]{:S(2)}, u32[]{:S(2)}) async-start(bf16[4,2,32768]{2,1,0:T(2,128)(2,1)} %reshape.271), calls=%async_computation.1 | async-start | bytes 1048576 | tf_op jit(solution)/shard_map/all_to_all | solution.py:45
  178.0 211.9 %copy-start.7 = (pred[128]{0:T(512)(128)(4,1)}, pred[128]{0:T(512)(128)(4,1)S(1)}, u32[]{:S(2)}) copy-start(pred[128]{0:T(512)(128)(4,1)S(1)} %get-tuple-element.6) | copy-start | bytes 388
  349.9 20.3 %all-to-all-start = ((bf16[4,2,65536]{2,1,0:T(2,128)(2,1)}), bf16[4,2,65536]{2,1,0:T(2,128)(2,1)S(1)}, u32[]{:S(2)}, u32[]{:S(2)}) async-start(bf16[4,2,65536]{2,1,0:T(2,128)(2,1)} %reshape.269), calls=%async_computation | async-start | bytes 2097152 | tf_op jit(solution)/shard_map/all_to_all | solution.py:44
  390.2 63.1 %collective-permute-start.1 = (bf16[8,4096]{1,0:T(8,128)(2,1)S(1)}, bf16[8,4096]{1,0:T(8,128)(2,1)S(1)}, u32[]{:S(2)}, u32[]{:S(2)}) collective-permute-start(bf16[8,4096]{1,0:T(8,128)(2,1)S(1)} %convolution_convert_fusion.1), channel_id=1, source_target_pairs={{0,128},{128,0},{1,129},{129,1},{2,130},{130,2},{3,131},{131,3},{4... | collective-permute-start | bytes 196616 | tf_op jit(solution)/shard_map/ppermute | solution.py:21
  459.5 13.5 %copy-start.8 = (pred[128]{0:T(512)(128)(4,1)S(1)}, pred[128]{0:T(512)(128)(4,1)}, u32[]{:S(2)}) copy-start(pred[128]{0:T(512)(128)(4,1)} %copy-done.7) | copy-start | bytes 388
  472.9 5.9 %copy-start.2 = (bf16[16,512,256]{1,2,0:T(8,128)(2,1)S(1)}, bf16[16,512,256]{1,2,0:T(8,128)(2,1)}, u32[]{:S(2)}) copy-start(bf16[16,512,256]{1,2,0:T(8,128)(2,1)} %convolution_convert_fusion.2) | copy-start | bytes 12582916
  472.9 5.9 %copy-start.3 = (bf16[64,64,512]{2,1,0:T(8,128)(2,1)S(1)}, bf16[64,64,512]{2,1,0:T(8,128)(2,1)}, u32[]{:S(2)}) copy-start(bf16[64,64,512]{2,1,0:T(8,128)(2,1)} %gather_fusion) | copy-start | bytes 12582916
  478.6 38.5 %collective-permute-start = (bf16[8,64,512]{2,1,0:T(8,128)(2,1)}, bf16[8,64,512]{2,1,0:T(8,128)(2,1)}, u32[]{:S(2)}, u32[]{:S(2)}) collective-permute-start(bf16[8,64,512]{2,1,0:T(8,128)(2,1)} %copy.129), channel_id=1, source_target_pairs={{0,128},{128,0},{1,129},{129,1},{2,130},{130,2},{3,131},{131,3},{4... | collective-permute-start | bytes 1572872 | tf_op jit(solution)/shard_map/ppermute | solution.py:21
  478.9 8.4 %copy-start.5 = (bf16[4,64,16,64]{3,2,1,0:T(8,128)(2,1)S(1)}, bf16[4,64,16,64]{3,2,1,0:T(8,128)(2,1)}, u32[]{:S(2)}) copy-start(bf16[4,64,16,64]{3,2,1,0:T(8,128)(2,1)} %reshape_squeeze.27) | copy-start | bytes 1572868
  500.0 19.6 %copy-start.1 = (bf16[16,128,512]{2,1,0:T(8,128)(2,1)S(1)}, bf16[16,128,512]{2,1,0:T(8,128)(2,1)}, u32[]{:S(2)}) copy-start(bf16[16,128,512]{2,1,0:T(8,128)(2,1)} %param.20) | copy-start | bytes 6291460
Sparse Core Ops, SparseCore 0:
  12.3 102.3 all-gather.4
  143.7 145.1 all-gather.2
Sparse Core Ops, SparseCore 1:
  139.3 180.1 all-reduce.1
where the time goes:
time: 537 us; the launch traced here: 527 us
  blocking collectives  230 us (43%)
  local copies, waits for them, and re-layouts  91 us (17%)
  other arithmetic  73.7 us (14%)
  starting transfers between devices  65.8 us (12%)
  matrix products  49.4 us (9%)
  between operations  16 us (3%)
    pmax x1, blocking collectives, body(): row_peak = lax.pmax(local_peak, 'ctx')  119 us
    psum x1, blocking collectives, body(): summed_mixture, summed_totals = lax.psum((dec_mixture, dec_totals), 'ctx')  111 us
    unnamed x2, other arithmetic  71 us
    ppermute x2, starting transfers between devices, swapped(): return lax.ppermute(block, axis, route)  57.1 us
    unnamed x32, local copies, waits for them, and re-layouts  32.9 us
    dot_general x1, matrix products, body(): jnp.einsum('bthl,hlv->bthv', mixture, w_uv, preferred_element_type=jnp.fl...  13.9 us
    another operation x1, local copies, waits for them, and re-layouts, body(): latent_blocks.reshape(block_count, BLK * LAT)  13.5 us
    sub x1, matrix products, body(): weights = jnp.where(allowed, jnp.exp(masked - peak_score), 0.0)  12.7 us
  transfers between devices with their start and end apart: 7, of which 0 were waited for; matrix products, arithmetic and copies ran while one was open for 35% of the time, Pallas kernels for 0%

commit v1 on v0

v1 whole, which is shorter than its diff:
```python
import functools

import jax
import jax.numpy as jnp
from jax import lax
from jax.experimental import pallas as pl
from jax.experimental.pallas import tpu as pltpu
from jax.sharding import Mesh, PartitionSpec as P

NOPE = 128
ROPE = 64
LAT = 512
VDIM = 128
BLK = 64
TOPK = 16
WIDE = LAT + 128
KEYS = TOPK * BLK
FEAT = 128
RROWS = BLK // 8
PART = BLK + RROWS
SET = TOPK * PART
LOW = -1e30
SCALE = (NOPE + ROPE) ** (-0.5)
SCALE2 = SCALE * 1.4426950408889634
F32 = jnp.float32
BF16 = jnp.bfloat16
NT = (((1,), (1,)), ((), ()))


PARAMS = pltpu.CompilerParams(vmem_limit_bytes=60 * 1024 * 1024)


def iota(shape, dim):
    return lax.broadcasted_iota(jnp.int32, shape, dim)


def whole(array):
    return pl.BlockSpec(array.shape, lambda *_: (0,) * len(array.shape))


SMALL = pl.BlockSpec(memory_space=pltpu.SMEM)


def unpaired(pairs):
    row, column = iota((BLK, BLK // 2), 0), iota((BLK, BLK // 2), 1)
    spread = jnp.where(row // 2 == column, 1.0, 0.0).astype(BF16)
    twice = jnp.dot(spread, pairs, preferred_element_type=F32)
    odd = iota((BLK, 128), 0) % 2 == 1
    return jnp.where(odd, pltpu.roll(twice, ROPE, 1), twice)


def slice_kernel(lat_ref, rope_ref, out_ref):
    count = lat_ref.shape[1] // FEAT
    tokens = unpaired(rope_ref[...])
    lane = iota((RROWS, 128), 1)
    for q in range(count):
        low = tokens[2 * q * RROWS : (2 * q + 1) * RROWS]
        high = tokens[(2 * q + 1) * RROWS : (2 * q + 2) * RROWS]
        rope = jnp.where(lane < ROPE, low, pltpu.roll(high, ROPE, 1)).astype(BF16)
        for z in range(out_ref.shape[0] // count):
            out_ref[z * count + q, :BLK] = lat_ref[:, q * FEAT : (q + 1) * FEAT]
            out_ref[z * count + q, BLK:] = rope


def slices(latent, rope, copies):
    out = jax.ShapeDtypeStruct((copies, PART, FEAT), BF16)
    return pl.pallas_call(
        slice_kernel,
        out_shape=out,
        grid=(1,),
        in_specs=[whole(latent), whole(rope)],
        out_specs=whole(out),
        compiler_params=PARAMS,
        name="slices",
    )(latent, rope)


def select_kernel(layout, code_ref, own_ref, near_ref, far_ref, back_ref, *refs):
    out_refs, all_ref = refs[:-1], refs[-1]
    start = 0
    for ref in (own_ref, near_ref, far_ref, back_ref):
        all_ref[start : start + ref.shape[0]] = ref[...]
        start += ref.shape[0]
    place = 0
    for sets, out_ref in zip(layout, out_refs):
        first = 0
        for blocks in sets:
            for j in range(0, blocks, 2):
                tails = []
                for i in (j, j + 1):
                    code = code_ref[place]
                    place += 1
                    source = jnp.maximum(code, 0)
                    lat = all_ref[source, :BLK]
                    tail = all_ref[source, BLK:].astype(F32)
                    if blocks < TOPK:
                        lat = jnp.where(code >= 0, lat, jnp.zeros_like(lat))
                        tail = jnp.where(code >= 0, tail, jnp.zeros_like(tail))
                    out_ref[first + i * BLK : first + (i + 1) * BLK] = lat
                    tails.append(tail)
                base = first + blocks * BLK + j * RROWS
                out_ref[base : base + 2 * RROWS] = jnp.concatenate(tails, axis=0).astype(BF16)
            first += blocks * PART


def select(codes, gathered, layout):
    sources = sum(part.shape[0] for part in gathered)
    outs = [jax.ShapeDtypeStruct((sum(sets) * PART, FEAT), BF16) for sets in layout]
    return pl.pallas_call(
        functools.partial(select_kernel, layout),
        out_shape=outs,
        grid=(1,),
        in_specs=[SMALL] + [whole(part) for part in gathered],
        out_specs=[whole(out) for out in outs],
        scratch_shapes=[pltpu.VMEM((sources, PART, FEAT), BF16)],
        compiler_params=PARAMS,
        name="select",
    )(codes, *gathered)


def quarter_of(me_ref, s):
    return lax.rem(me_ref[0] + 4 - me_ref[1] * s, 4)


def place_ropes(ref, quarter, rows):
    flat = rows.reshape(-1, 128)
    ref[:, 2 * quarter] = rows
    ref[:, 2 * quarter + 1] = pltpu.roll(flat, ROPE, 1).reshape(rows.shape)


def land_kernel(me_ref, *refs):
    parts = refs[:4]
    lat_ref, rope_ref, token_ref = refs[4:]
    slots = lat_ref.shape[0]
    for s, ref in enumerate(parts):
        q = quarter_of(me_ref, s)
        lat_ref[:, :, pl.ds(pl.multiple_of(q * FEAT, FEAT), FEAT)] = ref[: slots * BLK].reshape(
            slots, BLK, FEAT
        )
        place_ropes(token_ref, q, ref[slots * BLK :].astype(F32).reshape(slots, RROWS, 128))
    lane = iota((slots, 128), 1)
    for r in range(BLK // 2):
        octet, row = 2 * r // 8, 2 * r % 8
        even, odd = token_ref[:, octet, row, :], token_ref[:, octet, row + 1, :]
        both = jnp.where(lane < ROPE, even, pltpu.roll(odd, ROPE, 1))
        rope_ref[:, r * 128 : (r + 1) * 128] = both.astype(BF16)


def land(me, parts, slots):
    rows = slots * PART
    outs = (
        jax.ShapeDtypeStruct((slots, BLK, LAT), BF16),
        jax.ShapeDtypeStruct((slots, BLK * ROPE), BF16),
    )
    return pl.pallas_call(
        land_kernel,
        out_shape=outs,
        grid=(1,),
        in_specs=[SMALL] + [pl.BlockSpec((rows, FEAT), lambda c: (SET // rows, 0))] * len(parts),
        out_specs=tuple(whole(out) for out in outs),
        scratch_shapes=[pltpu.VMEM((slots, 8, 8, 128), F32)],
        compiler_params=PARAMS,
        name="land",
    )(me, *parts)


def split_kernel(me_ref, nope_ref, rope_ref, *out_refs):
    count = len(out_refs)
    nope, rope = nope_ref.shape[1] // count, rope_ref.shape[1] // count
    for s, out_ref in enumerate(out_refs):
        to = lax.rem(me_ref[0] + s, count)
        out_ref[:, :nope] = nope_ref[:, pl.ds(pl.multiple_of(to * nope, 128), nope)]
        out_ref[:, nope:] = rope_ref[:, pl.ds(pl.multiple_of(to * rope, 128), rope)]


def split(me, nope, rope, count):
    out = jax.ShapeDtypeStruct((nope.shape[0], (nope.shape[1] + rope.shape[1]) // count), BF16)
    return pl.pallas_call(
        split_kernel,
        out_shape=[out] * count,
        grid=(1,),
        in_specs=[SMALL, whole(nope), whole(rope)],
        out_specs=[whole(out)] * count,
        cost_estimate=pl.CostEstimate(
            flops=0, bytes_accessed=4 * (nope.size + rope.size), transcendentals=0
        ),
        compiler_params=PARAMS,
        name="split",
    )(me, nope, rope)


def absorb_kernel(order_ref, *refs):
    wuk_ref, out_ref = refs[-2:]
    blocks = out_ref.shape[0]
    nope = jnp.concatenate([ref[...] for ref in refs[:blocks]], axis=0)
    rope = jnp.concatenate([ref[...] for ref in refs[blocks : 2 * blocks]], axis=0).astype(F32)
    lane = iota((blocks * BLK, 128), 1)
    spot = iota((blocks * BLK, 128), 0) % BLK
    onehot = jnp.where(lane == spot + ROPE, 1.0, 0.0)
    for i in range(wuk_ref.shape[0]):
        part = rope[:, i // 2 * 128 : i // 2 * 128 + 128]
        if i % 2 == 1:
            part = pltpu.roll(part, ROPE, 1)
        tail = jnp.where(lane < ROPE, part, onehot).astype(BF16)
        absorbed = jnp.dot(
            nope[:, i * NOPE : (i + 1) * NOPE], wuk_ref[i], preferred_element_type=F32
        ).astype(BF16)
        rows = slice(i * BLK, (i + 1) * BLK)
        for b in range(blocks):
            out_ref[order_ref[b], rows, :LAT] = absorbed[b * BLK : (b + 1) * BLK]
            out_ref[order_ref[b], rows, LAT:] = tail[b * BLK : (b + 1) * BLK]


def absorb(order, queries, w_uk):
    blocks = len(queries)
    heads = w_uk.shape[0]
    some = 4
    rows = blocks * BLK * heads
    nope_spec = pl.BlockSpec((BLK, some * NOPE), lambda p: (0, p))
    rope_spec = pl.BlockSpec((BLK, some * ROPE), lambda p: (0, p + heads * NOPE // (some * ROPE)))
    return pl.pallas_call(
        absorb_kernel,
        out_shape=jax.ShapeDtypeStruct((blocks, heads * BLK, WIDE), BF16),
        grid=(heads // some,),
        in_specs=[SMALL]
        + [nope_spec] * blocks
        + [rope_spec] * blocks
        + [pl.BlockSpec((some, NOPE, LAT), lambda p: (p, 0, 0))],
        out_specs=pl.BlockSpec((blocks, some * BLK, WIDE), lambda p: (0, p, 0)),
        cost_estimate=pl.CostEstimate(
            flops=2 * rows * NOPE * LAT,
            bytes_accessed=rows * (WIDE + 192) * 2 + heads * NOPE * LAT * 2,
            transcendentals=0,
        ),
        compiler_params=PARAMS,
        name="absorb",
    )(order, *queries, *queries, w_uk)


def attend_kernel(mixed, ids_ref, block_ref, me_ref, *refs):
    set_refs, q_ref, refs = refs[:4], refs[4], refs[4:]
    mix_refs, wuv_ref = refs[1 : 1 + mixed], refs[-4]
    out_ref, keys_ref, token_ref = refs[-3:]

    @pl.when(pl.program_id(0) == 0)
    def _():
        for s, ref in enumerate(set_refs):
            quarter = quarter_of(me_ref, s)
            keys_ref[:, pl.ds(pl.multiple_of(quarter * FEAT, FEAT), FEAT)] = ref[:KEYS]
            place_ropes(token_ref, quarter, ref[KEYS:].astype(F32).reshape(TOPK, RROWS, 128))
        lane = iota((BLK, 128), 1)
        row = iota((BLK, 128), 0)
        place = block_ref[0] * BLK
        for j in range(TOPK):
            late = row + ids_ref[j] * BLK > place + lane - ROPE
            bias = jnp.where(late, LOW, 0.0)
            tail = jnp.where(lane < ROPE, token_ref[j].reshape(BLK, 128), bias)
            keys_ref[j * BLK : (j + 1) * BLK, LAT:] = tail.astype(BF16)

    rows = 4 * BLK
    chunks = [slice(at, at + rows) for at in range(0, q_ref.shape[1], rows)]
    scores = [
        lax.dot_general(q_ref[0, chunk, :], keys_ref[...], NT, preferred_element_type=F32)
        for chunk in chunks
    ]
    for chunk, s in zip(chunks, scores):
        peak = jnp.max(s, axis=1, keepdims=True)
        w = jnp.exp2((s - peak) * SCALE2)
        total = jnp.sum(w, axis=1, keepdims=True)
        o = jnp.dot(w.astype(BF16), keys_ref[:, :LAT], preferred_element_type=F32)
        o = (o * (1.0 / total)).astype(BF16)
        if mixed == 0:
            out_ref[chunk] = o
            continue
        for i in range(rows // BLK):
            h = chunk.start // BLK + i
            here = slice(h * BLK, (h + 1) * BLK)
            mixture = jnp.concatenate(
                [ref[here] for ref in mix_refs] + [o[i * BLK : (i + 1) * BLK]], axis=0
            )
            out_ref[:, h * VDIM : (h + 1) * VDIM] = jnp.dot(
                mixture, wuv_ref[h], preferred_element_type=F32
            ).astype(BF16)


def attend(index, sets, ids, block, me, q, mixtures=(), w_uv=None):
    rows = q.shape[1]
    steps = 2
    some = rows // steps
    operands = [ids, block, me, *sets, q]
    in_specs = (
        [SMALL] * 3
        + [pl.BlockSpec((SET, FEAT), lambda c: (0, 0))] * len(sets)
        + [pl.BlockSpec((1, some, WIDE), lambda c: (index, c, 0))]
    )
    if mixtures:
        tokens, heads = (len(mixtures) + 1) * BLK, w_uv.shape[0]
        operands += [*mixtures, w_uv]
        in_specs += [pl.BlockSpec((some, LAT), lambda c: (c, 0))] * len(mixtures)
        in_specs.append(pl.BlockSpec((heads // steps, LAT, VDIM), lambda c: (c, 0, 0)))
        out_shape = jax.ShapeDtypeStruct((tokens, heads * VDIM), BF16)
        out_spec = pl.BlockSpec((tokens, heads // steps * VDIM), lambda c: (0, c))
    else:
        out_shape = jax.ShapeDtypeStruct((rows, LAT), BF16)
        out_spec = pl.BlockSpec((some, LAT), lambda c: (c, 0))
    return pl.pallas_call(
        functools.partial(attend_kernel, len(mixtures)),
        out_shape=out_shape,
        grid=(steps,),
        in_specs=in_specs,
        out_specs=out_spec,
        scratch_shapes=[pltpu.VMEM((KEYS, WIDE), BF16), pltpu.VMEM((TOPK, 8, 8, 128), F32)],
        cost_estimate=pl.CostEstimate(
            flops=2 * rows * KEYS * (WIDE + LAT),
            bytes_accessed=rows * (WIDE + LAT) * 2 + 4 * SET * FEAT * 2,
            transcendentals=rows * KEYS,
        ),
        compiler_params=PARAMS,
        name="attend",
    )(*operands)


def decode_kernel(pages_ref, len_ref, first_ref, nope_ref, rope_ref, wuk_ref, wuv_ref,
                  lat_ref, keyrope_ref, out_ref, q_ref, mix_ref, stat_ref):
    heads = wuk_ref.shape[0]
    rows_total = nope_ref.shape[0]
    requests, pages = lat_ref.shape[0], lat_ref.shape[1]
    each = rows_total // requests
    local = pages * BLK
    lane = iota((rows_total, 128), 1)
    for h in range(heads):
        pair = rope_ref[:, h // 2 * 128 : h // 2 * 128 + 128].astype(F32)
        if h % 2 == 1:
            pair = pltpu.roll(pair, ROPE, 1)
        absorbed = jnp.dot(
            nope_ref[:, h * NOPE : (h + 1) * NOPE], wuk_ref[h], preferred_element_type=F32
        ).astype(BF16)
        tail = jnp.where(lane < ROPE, pair, 0.0).astype(BF16)
        for r in range(requests):
            q_ref[r, h * each : (h + 1) * each, :LAT] = absorbed[r * each : (r + 1) * each]
            q_ref[r, h * each : (h + 1) * each, LAT:] = tail[r * each : (r + 1) * each]
    first = first_ref[0]
    key_lane = iota((1, local), 1)
    for r in range(requests):
        usable = jnp.zeros((1, local), jnp.int32)
        for p in range(pages):
            page = first + p
            listed = pages_ref[r, 0] == page
            for j in range(1, pages_ref.shape[1]):
                listed = jnp.logical_or(listed, pages_ref[r, j] == page)
            filled = jnp.where(listed, jnp.clip(len_ref[r] - page * BLK, 0, BLK), 0)
            inside = (key_lane >= p * BLK) & (key_lane < p * BLK + filled)
            usable = jnp.where(inside, 1, usable)
        keep = usable > 0
        lat = lat_ref[r].reshape(local, LAT)
        tails = jnp.concatenate(
            [unpaired(keyrope_ref[r, p]) for p in range(pages)], axis=0
        )
        tails = jnp.where(iota((local, 128), 1) < ROPE, tails, 0.0).astype(BF16)
        s = lax.dot_general(q_ref[r, :, :LAT], lat, NT, preferred_element_type=F32)
        s = s + lax.dot_general(q_ref[r, :, LAT:], tails, NT, preferred_element_type=F32)
        s = jnp.where(keep, s, LOW)
        peak = jnp.max(s, axis=1, keepdims=True)
        peak_hi = peak.astype(BF16).astype(F32)
        peak_lo = (peak - peak_hi).astype(BF16).astype(F32)
        w = jnp.where(keep, jnp.exp2((s - (peak_hi + peak_lo)) * SCALE2), 0.0)
        total = jnp.sum(w, axis=1, keepdims=True)
        total_hi = total.astype(BF16).astype(F32)
        total_lo = total - total_hi
        o = jnp.dot(w.astype(BF16), lat, preferred_element_type=F32).astype(BF16)
        stat_lane = iota((heads * each, 128), 1)
        stat = jnp.where(stat_lane < 2 * heads, peak_hi, total_hi)
        low = jnp.where(stat_lane < 2 * heads, peak_lo, total_lo)
        stat = jnp.where(stat_lane % (2 * heads) < heads, stat, low)
        for h in range(heads):
            mix_ref[h, r * each : (r + 1) * each, :] = o[h * each : (h + 1) * each]
        merged = jnp.zeros((each, 128), F32)
        for h in range(heads):
            here = iota((each, 128), 1) % heads == h
            merged = jnp.where(here, stat[h * each : (h + 1) * each], merged)
        stat_ref[r * each : (r + 1) * each, :] = merged
    for h in range(heads):
        out_ref[:, h * VDIM : (h + 1) * VDIM] = jnp.dot(
            mix_ref[h], wuv_ref[h], preferred_element_type=F32
        ).astype(BF16)
    out_ref[:, heads * VDIM :] = stat_ref[...].astype(BF16)


def decode(page_lists, lengths, first, nope, rope, w_uk, w_uv, latents, ropes):
    rows = nope.shape[0]
    heads = w_uk.shape[0]
    requests = latents.shape[0]
    each = rows // requests
    operands = (nope, rope, w_uk, w_uv, latents, ropes)
    out = jax.ShapeDtypeStruct((rows, heads * VDIM + 128), BF16)
    return pl.pallas_call(
        decode_kernel,
        out_shape=out,
        grid=(1,),
        in_specs=[SMALL] * 3 + [whole(operand) for operand in operands],
        out_specs=whole(out),
        scratch_shapes=[
            pltpu.VMEM((requests, heads * each, WIDE), BF16),
            pltpu.VMEM((heads, rows, LAT), BF16),
            pltpu.VMEM((rows, 128), F32),
        ],
        cost_estimate=pl.CostEstimate(
            flops=1000000000, bytes_accessed=7 * 1024 * 1024, transcendentals=300000
        ),
        compiler_params=PARAMS,
        name="decode",
    )(page_lists, lengths, first, *operands)


def combine_kernel(parts_ref, out_ref):
    sources, rows = parts_ref.shape[0], parts_ref.shape[1]
    width = out_ref.shape[1]
    heads = width // VDIM
    for row in range(rows):
        part = parts_ref[:, row, :].astype(F32)
        stat = part[:, width:]
        peak = stat[:, :heads] + stat[:, heads : 2 * heads]
        total = stat[:, 2 * heads : 3 * heads] + stat[:, 3 * heads : 4 * heads]
        top = jnp.max(peak, axis=0, keepdims=True)
        factor = jnp.exp2((peak - top) * SCALE2)
        factor = factor / jnp.sum(factor * total, axis=0, keepdims=True)
        for h in range(heads):
            value = part[:, h * VDIM : (h + 1) * VDIM] * factor[:, h : h + 1]
            out_ref[row : row + 1, h * VDIM : (h + 1) * VDIM] = jnp.sum(
                value, axis=0, keepdims=True
            ).astype(BF16)


def combine(parts, width):
    out = jax.ShapeDtypeStruct((parts.shape[1], width), BF16)
    return pl.pallas_call(
        combine_kernel,
        out_shape=out,
        grid=(1,),
        in_specs=[whole(parts)],
        out_specs=whole(out),
        compiler_params=PARAMS,
        name="combine",
    )(parts)


def shifted(block, axis, distance):
    count = lax.axis_size(axis)
    return lax.ppermute(block, axis, [(i, (i + distance) % count) for i in range(count)])


def turned(block, axis, distance):
    count = lax.axis_size(axis)
    route = [
        (g * count + i, g * count + (i + (distance, -distance)[g]) % count)
        for g in (0, 1)
        for i in range(count)
    ]
    return lax.ppermute(block, ("grp", axis), route)


CTX = ("y", "z")


def after(value, *earlier):
    return lax.optimization_barrier((value, *earlier))[0]


def body(
    q_nope,
    q_rope,
    prompt_latent,
    prompt_rope,
    prompt_lists,
    owner_map,
    w_uk,
    w_uv,
    dec_nope,
    dec_rope,
    store_latent,
    store_rope,
    lengths,
    page_lists,
):
    y, z, me = lax.axis_index("y"), lax.axis_index("z"), lax.axis_index("hd")
    ys, zs, count = lax.axis_size("y"), lax.axis_size("z"), lax.axis_size("hd")
    ctx, contexts = y * zs + z, ys * zs
    block_count = contexts * count
    query_blocks = count
    turn = 1 - 2 * lax.axis_index("grp")
    here = me.reshape(1)
    ring = jnp.stack([me, turn])

    chunk = slices(prompt_latent[0], prompt_rope[0], zs * count)
    chunk = lax.all_to_all(chunk, ("z", "hd"), split_axis=0, concat_axis=0, tiled=True)

    requests, per_device = store_latent.shape[1], store_latent.shape[2]
    parts = decode(
        page_lists[0],
        lengths[0],
        (ctx * per_device).reshape(1),
        dec_nope[0],
        dec_rope[0],
        w_uk,
        w_uv,
        store_latent[0],
        store_rope[0].reshape(requests, per_device, BLK // 2, 128),
    )
    rows_total, wide = parts.shape
    parts = parts.reshape(contexts, rows_total // contexts, wide)

    shares = split(here, q_nope[0], q_rope[0], count)
    hop = turned(shares[2], "hd", 1)
    queries = [shares[0], shifted(shares[1], "hd", 1), None, shifted(shares[3], "hd", 3)]
    chunk = after(chunk, parts, hop, queries[1], queries[3])
    queries[2] = turned(hop, "hd", 1)
    near, back = turned(chunk, "y", 1), turned(chunk, "y", -1)
    far = turned(near, "y", 1)

    order = (me - jnp.arange(query_blocks, dtype=jnp.int32)) % count
    q = absorb(order, queries, w_uk)

    first_block = ctx * query_blocks
    listed = lax.dynamic_slice_in_dim(prompt_lists[0], first_block, query_blocks, 0)
    slot_count = 2 * block_count // contexts
    mine = (owner_map[0, :, 0] == ctx).astype(jnp.int32)
    ranking = jnp.cumsum(mine) - 1
    hit = (mine[None, :] == 1) & (
        ranking[None, :] == jnp.arange(slot_count, dtype=jnp.int32)[:, None]
    )
    pages = jnp.max(
        jnp.where(hit, jnp.arange(block_count, dtype=jnp.int32)[None, :], -1), axis=1
    )
    carrier = 2
    layout = [(TOPK,)] * query_blocks
    layout[carrier] = (TOPK, slot_count)
    wanted = jnp.concatenate(
        [listed[: carrier + 1].reshape(-1), pages, listed[carrier + 1 :].reshape(-1)]
    )
    row = zs * count
    codes = turn * (y - wanted // row) % ys * row + wanted % row
    codes = jnp.where(wanted < 0, -1, codes)

    parts = lax.all_to_all(parts, CTX, split_axis=0, concat_axis=0, tiled=True)
    dec_out = combine(parts, w_uv.shape[0] * VDIM)
    codes = after(codes, q, dec_out)
    sets = select(codes, (chunk, near, far, back), tuple(layout))

    rings, mixtures = [], []

    def mix(index, *ready):
        ids = after(listed[index], *ready)
        at = (first_block + index).reshape(1)
        mixtures.append(attend(index, rings[index], ids, at, ring, q))

    near_sets = []
    for index, block in enumerate(sets):
        if index >= 2:
            block = after(block, *near_sets[index - 2])
        near_sets.append((turned(block, "hd", 1), turned(block, "hd", -1)))
    for index, block in enumerate(sets):
        ahead, behind = near_sets[index]
        earlier = [rings[-1][2], mixtures[-1]] if index >= 2 else []
        far = turned(after(ahead, behind, *earlier), "hd", 1)
        rings.append((block, ahead, far, behind))
        if index in (1, 2):
            mix(index - 1, *near_sets[1])
    mix(2, mixtures[-1], *near_sets[3])
    landed = land(after(ring, mixtures[-1], rings[-1][2]), rings[carrier], slot_count)
    landed_latent, landed_rope = (lax.ppermute(x, "grp", [(0, 1), (1, 0)]) for x in landed)
    last = query_blocks - 1
    at = (first_block + last).reshape(1)
    pre_out = attend(last, rings[last], listed[last], at, ring, q, mixtures, w_uv)
    return (pre_out[None], dec_out[None], landed_latent[None], landed_rope[None])


def solution(mesh):
    mesh = Mesh(mesh.devices.reshape(2, 4, 8, 4), ("grp", *CTX, "hd"))
    in_specs = (
        P("grp", (*CTX, "hd"), None),
        P("grp", (*CTX, "hd"), None),
        P("grp", (*CTX, "hd"), None),
        P("grp", (*CTX, "hd"), None),
        P("grp", None, None),
        P("grp", None, None),
        P("hd", None, None),
        P("hd", None, None),
        P("grp", None, "hd"),
        P("grp", None, "hd"),
        P("grp", None, CTX, None, None),
        P("grp", None, CTX, None),
        P("grp", None),
        P("grp", None, None),
    )
    out_specs = (
        P("grp", CTX, "hd"),
        P("grp", CTX, "hd"),
        P("grp", CTX, None, None),
        P("grp", CTX, None),
    )
    return jax.shard_map(body, mesh=mesh, in_specs=in_specs, out_specs=out_specs, check_vma=False)
```

time: 537 us -> 140 us (0.26); the launches traced: 527 us -> 140 us
  blocking collectives: 230 us -> 0 us
  local copies, waits for them, and re-layouts: 91 us -> 8.19 us
  other arithmetic: 73.7 us -> 2.25 us
  Pallas kernels: 0 us -> 50.6 us
  matrix products: 49.4 us -> 0 us
  waiting for transfers between devices: 1.43 us -> 26.6 us
  between operations: 16 us -> 0.83 us
  starting transfers between devices: 65.8 us -> 51.3 us
    pmax x1 -> x0, blocking collectives: 119 us -> none  [body(): row_peak = lax.pmax(local_peak, 'ctx')]
    psum x1 -> x0, blocking collectives: 111 us -> none  [body(): summed_mixture, summed_totals = lax.psum((dec_mixture, dec_totals), 'ctx')]
    unnamed x2 -> x0, other arithmetic: 71 us -> none
    pallas_call x0 -> x11, Pallas kernels: none -> 50.6 us  [the longest x4 25.8 us: attend(): pl.pallas_call(functools.partial(attend_kernel, len(mixtures)), out_shape...]
    dot_general x10 -> x0, matrix products: 36.6 us -> none  [the longest x1 13.9 us: body(): jnp.einsum('bthl,hlv->bthv', mixture, w_uv, preferred_element_type=jnp.fl...]
    unnamed x32 -> x52, local copies, waits for them, and re-layouts: 32.9 us -> 4.48 us
    ppermute x2 -> x21, waiting for transfers between devices: 0.01 us -> 26.4 us  [the longest x17 20.7 us: turned(): return lax.ppermute(block, ('grp', axis), route)]
    ppermute x2 -> x21, starting transfers between devices: 57.1 us -> 33.6 us  [the longest x17 28.2 us: turned(): return lax.ppermute(block, ('grp', axis), route)]
  transfers between devices with their start and end apart: 7 -> 23, of which waited for: 0 -> 10; matrix products, arithmetic and copies ran while one was open for 35% -> 4% of each run, Pallas kernels for 0% -> 31%
where the time goes in v1:
time: 140 us
  starting transfers between devices  51.3 us (37%)
  Pallas kernels  50.6 us (36%)
  waiting for transfers between devices  26.6 us (19%)
  local copies, waits for them, and re-layouts  8.19 us (6%)
  other arithmetic  2.25 us (2%)
    ppermute x17, starting transfers between devices, turned(): return lax.ppermute(block, ('grp', axis), route)  28.2 us
    pallas_call x4, Pallas kernels, attend(): pl.pallas_call(functools.partial(attend_kernel, len(mixtures)), out_shape...  25.8 us
    ppermute x17, waiting for transfers between devices, turned(): return lax.ppermute(block, ('grp', axis), route)  20.7 us
    all_to_all x1, starting transfers between devices, body(): lax.all_to_all(chunk, ('z', 'hd'), split_axis=0, concat_axis=0, tiled=True)  11.9 us
    pallas_call x1, Pallas kernels, decode(): pl.pallas_call(decode_kernel, out_shape=out, grid=(1,), in_specs=[SMALL]...  7.11 us
    all_to_all x1, starting transfers between devices, body(): parts = lax.all_to_all(parts, CTX, split_axis=0, concat_axis=0, tiled=True)  5.86 us
    pallas_call x1, Pallas kernels, absorb(): pl.pallas_call(absorb_kernel, out_shape=jax.ShapeDtypeStruct((blocks, hea...  5.85 us
    ppermute x2, waiting for transfers between devices, shifted(): lax.ppermute(block, axis, [(i, (i + distance) % count) for i in range(cou...  5.7 us
  transfers between devices with their start and end apart: 23, of which 10 were waited for; matrix products, arithmetic and copies ran while one was open for 4% of the time, Pallas kernels for 31%

profile of v1, /device:TPU:1, one launch (start us, length us, event | category | flops | bytes accessed | tf_op | source)
XLA Modules:
  0.0 139.8 jit_solution(9540653807180269792)
XLA Ops:
  2.6 11.9 %all-to-all-start.1 = ((bf16[32,72,128]{2,1,0:T(8,128)(2,1)}), bf16[32,72,128]{2,1,0:T(8,128)(2,1)S(1)}, u32[]{:S(2)}, u32[]{:S(2)}) async-start(bf16[32,72,128]{2,1,0:T(8,128)(2,1)} %slices.1), calls=%async_computation.1 | async-start | bytes 1179648 | tf_op jit(solution)/shard_map/all_to_all | solution.py:495
  14.5 2.6 %split.1 = (bf16[64,3072]{1,0:T(8,128)(2,1)}, bf16[64,3072]{1,0:T(8,128)(2,1)}, bf16[64,3072]{1,0:T(8,128)(2,1)}, bf16[64,3072]{1,0:T(8,128)(2,1)}) custom-call(s32[1]{0:T(128)} %bitcast.1.me_ref, bf16[64,8192]{1,0:T(8,128)(2,1)} %bitcast.24, bf16[64,4096]{1,0:T(8,128)(2,1)} %bitcast.26), custom_call_target="tpu_custom_call" | custom-call | bytes 3145728 | tf_op jit(solution)/shard_map/split/pallas_call | solution.py:178
  19.5 2.7 %collective-permute-start.3 = (bf16[64,3072]{1,0:T(8,128)(2,1)}, bf16[64,3072]{1,0:T(8,128)(2,1)S(1)}, u32[]{:S(2)}, u32[]{:S(2)}) collective-permute-start(bf16[64,3072]{1,0:T(8,128)(2,1)} %get-tuple-element.29), channel_id=1, source_target_pairs={{0,3},{1,0},{2,1},{3,2},{4,7},{5,4},{6,5},{7,6},{8,11},{9,8},{10,9... | collective-permute-start | bytes 1179656 | tf_op jit(solution)/shard_map/ppermute | solution.py:449
  23.0 7.1 %decode.1 = bf16[64,2176]{1,0:T(8,128)(2,1)} custom-call(s32[4,16]{1,0:T(4,128)} %bitcast.34, s32[4]{0:T(128)} %bitcast.35, s32[1]{0:T(128)} %bitcast.9.first_ref.block_ref, bf16[64,2048]{1,0:T(8,128)(2,1)} %bitcast.28, bf16[64,1024]{1,0:T(8,128)(2,1)} %bitcast.29, bf16[16,128,512]{2,1,0:T(8,128)(2,1)} %wuk_ref.1, bf16[16,512,128]{2,1,0:T(8,128)(2,1)} %refs_8_.3, ...), custom_call_target="tpu_custom_call" | custom-call | flops 1000000000 | bytes 7340032 | tf_op jit(solution)/shard_map/decode/pallas_call | solution.py:396
  31.9 4.5 %collective-permute-done.refs_1_.refs_5_ = bf16[64,3072]{1,0:T(8,128)(2,1)S(1)} collective-permute-done((bf16[64,3072]{1,0:T(8,128)(2,1)}, bf16[64,3072]{1,0:T(8,128)(2,1)S(1)}, u32[]{:S(2)}, u32[]{:S(2)}) %collective-permute-start) | collective-permute-done | bytes 393248 | tf_op jit(solution)/shard_map/ppermute | solution.py:449
  37.6 2.8 %collective-permute-start.4 = (bf16[32,72,128]{2,1,0:T(8,128)(2,1)S(1)}, bf16[32,72,128]{2,1,0:T(8,128)(2,1)S(1)}, u32[]{:S(2)}, u32[]{:S(2)}) collective-permute-start(bf16[32,72,128]{2,1,0:T(8,128)(2,1)S(1)} %all-to-all-done.1.own_ref), channel_id=1, source_target_pairs={{0,32},{32,64},{64,96},{96,0},{128,224},{160,128},{192,160},{224,1... | collective-permute-start | bytes 1769480 | tf_op jit(solution)/shard_map/ppermute | solution.py:459
  40.4 5.9 %all-to-all-start = ((bf16[32,2,2176]{2,1,0:T(2,128)(2,1)}), bf16[32,2,2176]{2,1,0:T(2,128)(2,1)S(1)}, u32[]{:S(2)}, u32[]{:S(2)}) async-start(bf16[32,2,2176]{2,1,0:T(2,128)(2,1)} %reshape.96), calls=%async_computation | async-start | bytes 557056 | tf_op jit(solution)/shard_map/all_to_all | solution.py:544
  47.7 2.7 %collective-permute-start.5 = (bf16[32,72,128]{2,1,0:T(8,128)(2,1)S(1)}, bf16[32,72,128]{2,1,0:T(8,128)(2,1)}, u32[]{:S(2)}, u32[]{:S(2)}) collective-permute-start(bf16[32,72,128]{2,1,0:T(8,128)(2,1)S(1)} %collective-permute-done.4.near_ref), channel_id=1, source_target_pairs={{0,32},{32,64},{64,96},{96,0},{128,224},{160,128},{192,160},{224,1... | collective-permute-start | bytes 1769480 | tf_op jit(solution)/shard_map/ppermute | solution.py:459
  50.5 2.6 %collective-permute-start.2 = (bf16[64,3072]{1,0:T(8,128)(2,1)}, bf16[64,3072]{1,0:T(8,128)(2,1)S(1)}, u32[]{:S(2)}, u32[]{:S(2)}) collective-permute-start(bf16[64,3072]{1,0:T(8,128)(2,1)} %copy-done.18), channel_id=1, source_target_pairs={{0,1},{1,2},{2,3},{3,0},{128,131},{129,128},{130,129},{131,130},{4... | collective-permute-start | bytes 1179656 | tf_op jit(solution)/shard_map/ppermute | solution.py:459
  59.5 5.8 %absorb.1.refs_4_ = bf16[4,1024,640]{2,1,0:T(8,128)(2,1)} custom-call(s32[4]{0:T(128)} %and_select_fusion.order_ref, bf16[64,3072]{1,0:T(8,128)(2,1)} %get-tuple-element.26.refs_0_.refs_4_, bf16[64,3072]{1,0:T(8,128)(2,1)} %copy-done.1, bf16[64,3072]{1,0:T(8,128)(2,1)} %copy-done.3, bf16[64,3072]{1,0:T(8,128)(2,1)} %copy-done.2, ...), custom_call_target="tpu_custom_call" | custom-call | flops 536870912 | bytes 8912896 | tf_op jit(solution)/shard_map/absorb/pallas_call | solution.py:221
  66.2 2.8 %select.11 = (bf16[1152,128]{1,0:T(8,128)(2,1)}, bf16[1152,128]{1,0:T(8,128)(2,1)}, bf16[1728,128]{1,0:T(8,128)(2,1)}, bf16[1152,128]{1,0:T(8,128)(2,1)}) custom-call(s32[72]{0:T(128)} %fusion.2.code_ref, bf16[32,72,128]{2,1,0:T(8,128)(2,1)} %copy-done, bf16[32,72,128]{2,1,0:T(8,128)(2,1)} %copy-done.5, bf16[32,72,128]{2,1,0:T(8,128)(2,1)} %collective-permute-done.5.far_ref, ...), custom_call_target="tpu_custom_call" | custom-call | tf_op jit(solution)/shard_map/select/pallas_call | solution.py:109
  69.1 2.8 %collective-permute-start.11 = (bf16[1152,128]{1,0:T(8,128)(2,1)}, bf16[1152,128]{1,0:T(8,128)(2,1)S(1)}, u32[]{:S(2)}, u32[]{:S(2)}) collective-permute-start(bf16[1152,128]{1,0:T(8,128)(2,1)} %get-tuple-element.36.refs_0_), channel_id=1, source_target_pairs={{0,1},{1,2},{2,3},{3,0},{128,131},{129,128},{130,129},{131,130},{4... | collective-permute-start | bytes 884744 | tf_op jit(solution)/shard_map/ppermute | solution.py:459
  71.8 2.7 %collective-permute-start.7 = (bf16[1152,128]{1,0:T(8,128)(2,1)}, bf16[1152,128]{1,0:T(8,128)(2,1)S(1)}, u32[]{:S(2)}, u32[]{:S(2)}) collective-permute-start(bf16[1152,128]{1,0:T(8,128)(2,1)} %get-tuple-element.33.refs_0_), channel_id=1, source_target_pairs={{0,1},{1,2},{2,3},{3,0},{128,131},{129,128},{130,129},{131,130},{4... | collective-permute-start | bytes 884744 | tf_op jit(solution)/shard_map/ppermute | solution.py:459
  75.8 3.0 %collective-permute-done.12.refs_3_ = bf16[1152,128]{1,0:T(8,128)(2,1)S(1)} collective-permute-done((bf16[1152,128]{1,0:T(8,128)(2,1)}, bf16[1152,128]{1,0:T(8,128)(2,1)S(1)}, u32[]{:S(2)}, u32[]{:S(2)}) %collective-permute-start.12) | collective-permute-done | bytes 294944 | tf_op jit(solution)/shard_map/ppermute | solution.py:459
  80.4 4.9 %collective-permute-done.8.refs_3_ = bf16[1152,128]{1,0:T(8,128)(2,1)S(1)} collective-permute-done((bf16[1152,128]{1,0:T(8,128)(2,1)}, bf16[1152,128]{1,0:T(8,128)(2,1)S(1)}, u32[]{:S(2)}, u32[]{:S(2)}) %collective-permute-start.8) | collective-permute-done | bytes 294944 | tf_op jit(solution)/shard_map/ppermute | solution.py:459
  88.5 5.9 %attend.4.refs_5_ = bf16[1024,512]{1,0:T(8,128)(2,1)} custom-call(s32[16]{0:T(128)} %get-tuple-element.39.ids_ref, s32[1]{0:T(128)} %bitcast.9.first_ref.block_ref, s32[2]{0:T(128)} %pad_add_fusion.me_ref, bf16[1152,128]{1,0:T(8,128)(2,1)} %get-tuple-element.36.refs_0_, bf16[1152,128]{1,0:T(8,128)(2,1)} %copy-done.21, bf16[1152,128]{1,0:T(8,128)(2,1)} %copy-done.24, ...), custom_call_target="tpu_custom_call" | custom-call | flops 2415919104 | bytes 3538944 | tf_op jit(solution)/shard_map/attend/pallas_call | solution.py:306
  94.4 6.6 %collective-permute-done.15.refs_2_ = bf16[1152,128]{1,0:T(8,128)(2,1)S(1)} collective-permute-done((bf16[1152,128]{1,0:T(8,128)(2,1)S(1)}, bf16[1152,128]{1,0:T(8,128)(2,1)S(1)}, u32[]{:S(2)}, u32[]{:S(2)}) %collective-permute-start.15) | collective-permute-done | bytes 294944 | tf_op jit(solution)/shard_map/ppermute | solution.py:459
  101.0 3.2 %collective-permute-start.17 = (bf16[1728,128]{1,0:T(8,128)(2,1)S(1)}, bf16[1728,128]{1,0:T(8,128)(2,1)S(1)}, u32[]{:S(2)}, u32[]{:S(2)}) collective-permute-start(bf16[1728,128]{1,0:T(8,128)(2,1)S(1)} %collective-permute-done.13.refs_1_), channel_id=1, source_target_pairs={{0,1},{1,2},{2,3},{3,0},{128,131},{129,128},{130,129},{131,130},{4... | collective-permute-start | bytes 1327112 | tf_op jit(solution)/shard_map/ppermute | solution.py:459
  104.2 2.7 %collective-permute-start.9 = (bf16[1152,128]{1,0:T(8,128)(2,1)S(1)}, bf16[1152,128]{1,0:T(8,128)(2,1)S(1)}, u32[]{:S(2)}, u32[]{:S(2)}) collective-permute-start(bf16[1152,128]{1,0:T(8,128)(2,1)S(1)} %copy-done.10), channel_id=1, source_target_pairs={{0,1},{1,2},{2,3},{3,0},{128,131},{129,128},{130,129},{131,130},{4... | collective-permute-start | bytes 884744 | tf_op jit(solution)/shard_map/ppermute | solution.py:459
  106.9 5.9 %attend.5.refs_6_ = bf16[1024,512]{1,0:T(8,128)(2,1)} custom-call(s32[16]{0:T(128)} %get-tuple-element.42.ids_ref, s32[1]{0:T(128)} %bitcast.15.block_ref, s32[2]{0:T(128)} %pad_add_fusion.me_ref, bf16[1152,128]{1,0:T(8,128)(2,1)} %get-tuple-element.33.refs_0_, bf16[1152,128]{1,0:T(8,128)(2,1)} %copy-done.19, bf16[1152,128]{1,0:T(8,128)(2,1)} %copy-done.23, ...), custom_call_target="tpu_custom_call" | custom-call | flops 2415919104 | bytes 3538944 | tf_op jit(solution)/shard_map/attend/pallas_call | solution.py:306
  115.8 3.4 %collective-permute-start.18 = (bf16[1152,128]{1,0:T(8,128)(2,1)S(1)}, bf16[1152,128]{1,0:T(8,128)(2,1)S(1)}, u32[]{:S(2)}, u32[]{:S(2)}) collective-permute-start(bf16[1152,128]{1,0:T(8,128)(2,1)S(1)} %collective-permute-done.9.refs_1_), channel_id=1, source_target_pairs={{0,1},{1,2},{2,3},{3,0},{128,131},{129,128},{130,129},{131,130},{4... | collective-permute-start | bytes 884744 | tf_op jit(solution)/shard_map/ppermute | solution.py:459
  119.2 5.9 %attend.6.refs_7_ = bf16[1024,512]{1,0:T(8,128)(2,1)} custom-call(s32[16]{0:T(128)} %get-tuple-element.44.ids_ref, s32[1]{0:T(128)} %bitcast.16.block_ref, s32[2]{0:T(128)} %pad_add_fusion.me_ref, bf16[1728,128]{1,0:T(8,128)(2,1)} %get-tuple-element.37.refs_0_, bf16[1728,128]{1,0:T(8,128)(2,1)} %copy-done.7, bf16[1728,128]{1,0:T(8,128)(2,1)} %copy-done.9, ...), custom_call_target="tpu_custom_call" | custom-call | flops 2415919104 | bytes 3538944 | tf_op jit(solution)/shard_map/attend/pallas_call | solution.py:306
  127.5 2.7 %collective-permute-start.19 = (bf16[8,64,512]{2,1,0:T(8,128)(2,1)}, bf16[8,64,512]{2,1,0:T(8,128)(2,1)S(1)}, u32[]{:S(2)}, u32[]{:S(2)}) collective-permute-start(bf16[8,64,512]{2,1,0:T(8,128)(2,1)} %get-tuple-element.46), channel_id=1, source_target_pairs={{0,128},{128,0},{1,129},{129,1},{2,130},{130,2},{3,131},{131,3},{4... | collective-permute-start | bytes 1572872 | tf_op jit(solution)/shard_map/ppermute | solution.py:570
  130.2 8.1 %attend.7 = bf16[256,2048]{1,0:T(8,128)(2,1)} custom-call(s32[16]{0:T(128)} %copy-done.16, s32[1]{0:T(128)} %bitcast.block_ref, s32[2]{0:T(128)} %pad_add_fusion.me_ref, bf16[1152,128]{1,0:T(8,128)(2,1)} %get-tuple-element.34.refs_0_, bf16[1152,128]{1,0:T(8,128)(2,1)} %copy-done.12, bf16[1152,128]{1,0:T(8,128)(2,1)} %copy-done.13, ...), custom_call_target="tpu_custom_call" | custom-call | flops 2415919104 | bytes 3538944 | tf_op jit(solution)/shard_map/attend/pallas_call | solution.py:306
  (99 shorter events, 29.8 us)
Async XLA Ops:
  2.6 35.0 %all-to-all-start.1 = ((bf16[32,72,128]{2,1,0:T(8,128)(2,1)}), bf16[32,72,128]{2,1,0:T(8,128)(2,1)S(1)}, u32[]{:S(2)}, u32[]{:S(2)}) async-start(bf16[32,72,128]{2,1,0:T(8,128)(2,1)} %slices.1), calls=%async_computation.1 | async-start | bytes 1179648 | tf_op jit(solution)/shard_map/all_to_all | solution.py:495
  17.1 14.8 %collective-permute-start.1 = (bf16[64,3072]{1,0:T(8,128)(2,1)}, bf16[64,3072]{1,0:T(8,128)(2,1)S(1)}, u32[]{:S(2)}, u32[]{:S(2)}) collective-permute-start(bf16[64,3072]{1,0:T(8,128)(2,1)} %get-tuple-element.28), channel_id=1, source_target_pairs={{0,1},{1,2},{2,3},{3,0},{128,131},{129,128},{130,129},{131,130},{4... | collective-permute-start | bytes 1179656 | tf_op jit(solution)/shard_map/ppermute | solution.py:459
  19.5 16.8 %collective-permute-start = (bf16[64,3072]{1,0:T(8,128)(2,1)}, bf16[64,3072]{1,0:T(8,128)(2,1)S(1)}, u32[]{:S(2)}, u32[]{:S(2)}) collective-permute-start(bf16[64,3072]{1,0:T(8,128)(2,1)} %get-tuple-element.27), channel_id=1, source_target_pairs={{0,1},{1,2},{2,3},{3,0},{4,5},{5,6},{6,7},{7,4},{8,9},{9,10},{10,1... | collective-permute-start | bytes 1179656 | tf_op jit(solution)/shard_map/ppermute | solution.py:449
  19.5 18.1 %collective-permute-start.3 = (bf16[64,3072]{1,0:T(8,128)(2,1)}, bf16[64,3072]{1,0:T(8,128)(2,1)S(1)}, u32[]{:S(2)}, u32[]{:S(2)}) collective-permute-start(bf16[64,3072]{1,0:T(8,128)(2,1)} %get-tuple-element.29), channel_id=1, source_target_pairs={{0,3},{1,0},{2,1},{3,2},{4,7},{5,4},{6,5},{7,6},{8,11},{9,8},{10,9... | collective-permute-start | bytes 1179656 | tf_op jit(solution)/shard_map/ppermute | solution.py:449
  37.6 27.8 %copy-start = (bf16[32,72,128]{2,1,0:T(8,128)(2,1)}, bf16[32,72,128]{2,1,0:T(8,128)(2,1)S(1)}, u32[]{:S(2)}) copy-start(bf16[32,72,128]{2,1,0:T(8,128)(2,1)S(1)} %all-to-all-done.1.own_ref) | copy-start | bytes 1769476
  37.6 10.0 %collective-permute-start.4 = (bf16[32,72,128]{2,1,0:T(8,128)(2,1)S(1)}, bf16[32,72,128]{2,1,0:T(8,128)(2,1)S(1)}, u32[]{:S(2)}, u32[]{:S(2)}) collective-permute-start(bf16[32,72,128]{2,1,0:T(8,128)(2,1)S(1)} %all-to-all-done.1.own_ref), channel_id=1, source_target_pairs={{0,32},{32,64},{64,96},{96,0},{128,224},{160,128},{192,160},{224,1... | collective-permute-start | bytes 1769480 | tf_op jit(solution)/shard_map/ppermute | solution.py:459
  40.4 15.6 %all-to-all-start = ((bf16[32,2,2176]{2,1,0:T(2,128)(2,1)}), bf16[32,2,2176]{2,1,0:T(2,128)(2,1)S(1)}, u32[]{:S(2)}, u32[]{:S(2)}) async-start(bf16[32,2,2176]{2,1,0:T(2,128)(2,1)} %reshape.96), calls=%async_computation | async-start | bytes 557056 | tf_op jit(solution)/shard_map/all_to_all | solution.py:544
  46.3 19.0 %collective-permute-start.6 = (bf16[32,72,128]{2,1,0:T(8,128)(2,1)S(1)}, bf16[32,72,128]{2,1,0:T(8,128)(2,1)S(1)}, u32[]{:S(2)}, u32[]{:S(2)}) collective-permute-start(bf16[32,72,128]{2,1,0:T(8,128)(2,1)S(1)} %all-to-all-done.1.own_ref), channel_id=1, source_target_pairs={{0,96},{32,0},{64,32},{96,64},{128,160},{160,192},{192,224},{224,1... | collective-permute-start | bytes 1769480 | tf_op jit(solution)/shard_map/ppermute | solution.py:459
  47.7 17.7 %collective-permute-start.5 = (bf16[32,72,128]{2,1,0:T(8,128)(2,1)S(1)}, bf16[32,72,128]{2,1,0:T(8,128)(2,1)}, u32[]{:S(2)}, u32[]{:S(2)}) collective-permute-start(bf16[32,72,128]{2,1,0:T(8,128)(2,1)S(1)} %collective-permute-done.4.near_ref), channel_id=1, source_target_pairs={{0,32},{32,64},{64,96},{96,0},{128,224},{160,128},{192,160},{224,1... | collective-permute-start | bytes 1769480 | tf_op jit(solution)/shard_map/ppermute | solution.py:459
  50.5 8.3 %collective-permute-start.2 = (bf16[64,3072]{1,0:T(8,128)(2,1)}, bf16[64,3072]{1,0:T(8,128)(2,1)S(1)}, u32[]{:S(2)}, u32[]{:S(2)}) collective-permute-start(bf16[64,3072]{1,0:T(8,128)(2,1)} %copy-done.18), channel_id=1, source_target_pairs={{0,1},{1,2},{2,3},{3,0},{128,131},{129,128},{130,129},{131,130},{4... | collective-permute-start | bytes 1179656 | tf_op jit(solution)/shard_map/ppermute | solution.py:459
  69.1 6.8 %collective-permute-start.11 = (bf16[1152,128]{1,0:T(8,128)(2,1)}, bf16[1152,128]{1,0:T(8,128)(2,1)S(1)}, u32[]{:S(2)}, u32[]{:S(2)}) collective-permute-start(bf16[1152,128]{1,0:T(8,128)(2,1)} %get-tuple-element.36.refs_0_), channel_id=1, source_target_pairs={{0,1},{1,2},{2,3},{3,0},{128,131},{129,128},{130,129},{131,130},{4... | collective-permute-start | bytes 884744 | tf_op jit(solution)/shard_map/ppermute | solution.py:459
  71.8 7.0 %collective-permute-start.12 = (bf16[1152,128]{1,0:T(8,128)(2,1)}, bf16[1152,128]{1,0:T(8,128)(2,1)S(1)}, u32[]{:S(2)}, u32[]{:S(2)}) collective-permute-start(bf16[1152,128]{1,0:T(8,128)(2,1)} %get-tuple-element.36.refs_0_), channel_id=1, source_target_pairs={{0,3},{1,0},{2,1},{3,2},{128,129},{129,130},{130,131},{131,128},{4... | collective-permute-start | bytes 884744 | tf_op jit(solution)/shard_map/ppermute | solution.py:459
  71.8 8.5 %collective-permute-start.7 = (bf16[1152,128]{1,0:T(8,128)(2,1)}, bf16[1152,128]{1,0:T(8,128)(2,1)S(1)}, u32[]{:S(2)}, u32[]{:S(2)}) collective-permute-start(bf16[1152,128]{1,0:T(8,128)(2,1)} %get-tuple-element.33.refs_0_), channel_id=1, source_target_pairs={{0,1},{1,2},{2,3},{3,0},{128,131},{129,128},{130,129},{131,130},{4... | collective-permute-start | bytes 884744 | tf_op jit(solution)/shard_map/ppermute | solution.py:459
  74.5 10.7 %collective-permute-start.8 = (bf16[1152,128]{1,0:T(8,128)(2,1)}, bf16[1152,128]{1,0:T(8,128)(2,1)S(1)}, u32[]{:S(2)}, u32[]{:S(2)}) collective-permute-start(bf16[1152,128]{1,0:T(8,128)(2,1)} %get-tuple-element.33.refs_0_), channel_id=1, source_target_pairs={{0,3},{1,0},{2,1},{3,2},{128,129},{129,130},{130,131},{131,128},{4... | collective-permute-start | bytes 884744 | tf_op jit(solution)/shard_map/ppermute | solution.py:459
  78.8 8.9 %collective-permute-start.16 = (bf16[1152,128]{1,0:T(8,128)(2,1)S(1)}, bf16[1152,128]{1,0:T(8,128)(2,1)S(1)}, u32[]{:S(2)}, u32[]{:S(2)}) collective-permute-start(bf16[1152,128]{1,0:T(8,128)(2,1)S(1)} %collective-permute-done.11.refs_1_), channel_id=1, source_target_pairs={{0,1},{1,2},{2,3},{3,0},{128,131},{129,128},{130,129},{131,130},{4... | collective-permute-start | bytes 884744 | tf_op jit(solution)/shard_map/ppermute | solution.py:459
  78.9 22.1 %collective-permute-start.13 = (bf16[1728,128]{1,0:T(8,128)(2,1)}, bf16[1728,128]{1,0:T(8,128)(2,1)S(1)}, u32[]{:S(2)}, u32[]{:S(2)}) collective-permute-start(bf16[1728,128]{1,0:T(8,128)(2,1)} %get-tuple-element.37.refs_0_), channel_id=1, source_target_pairs={{0,1},{1,2},{2,3},{3,0},{128,131},{129,128},{130,129},{131,130},{4... | collective-permute-start | bytes 1327112 | tf_op jit(solution)/shard_map/ppermute | solution.py:459
  79.0 22.0 %collective-permute-start.14 = (bf16[1728,128]{1,0:T(8,128)(2,1)}, bf16[1728,128]{1,0:T(8,128)(2,1)S(1)}, u32[]{:S(2)}, u32[]{:S(2)}) collective-permute-start(bf16[1728,128]{1,0:T(8,128)(2,1)} %get-tuple-element.37.refs_0_), channel_id=1, source_target_pairs={{0,3},{1,0},{2,1},{3,2},{128,129},{129,130},{130,131},{131,128},{4... | collective-permute-start | bytes 1327112 | tf_op jit(solution)/shard_map/ppermute | solution.py:459
  85.2 15.7 %collective-permute-start.15 = (bf16[1152,128]{1,0:T(8,128)(2,1)S(1)}, bf16[1152,128]{1,0:T(8,128)(2,1)S(1)}, u32[]{:S(2)}, u32[]{:S(2)}) collective-permute-start(bf16[1152,128]{1,0:T(8,128)(2,1)S(1)} %collective-permute-done.7.refs_1_), channel_id=1, source_target_pairs={{0,1},{1,2},{2,3},{3,0},{128,131},{129,128},{130,129},{131,130},{4... | collective-permute-start | bytes 884744 | tf_op jit(solution)/shard_map/ppermute | solution.py:459
  101.0 14.8 %collective-permute-start.17 = (bf16[1728,128]{1,0:T(8,128)(2,1)S(1)}, bf16[1728,128]{1,0:T(8,128)(2,1)S(1)}, u32[]{:S(2)}, u32[]{:S(2)}) collective-permute-start(bf16[1728,128]{1,0:T(8,128)(2,1)S(1)} %collective-permute-done.13.refs_1_), channel_id=1, source_target_pairs={{0,1},{1,2},{2,3},{3,0},{128,131},{129,128},{130,129},{131,130},{4... | collective-permute-start | bytes 1327112 | tf_op jit(solution)/shard_map/ppermute | solution.py:459
  104.2 9.1 %collective-permute-start.10 = (bf16[1152,128]{1,0:T(8,128)(2,1)S(1)}, bf16[1152,128]{1,0:T(8,128)(2,1)S(1)}, u32[]{:S(2)}, u32[]{:S(2)}) collective-permute-start(bf16[1152,128]{1,0:T(8,128)(2,1)S(1)} %copy-done.10), channel_id=1, source_target_pairs={{0,3},{1,0},{2,1},{3,2},{128,129},{129,130},{130,131},{131,128},{4... | collective-permute-start | bytes 884744 | tf_op jit(solution)/shard_map/ppermute | solution.py:459
  104.2 11.6 %collective-permute-start.9 = (bf16[1152,128]{1,0:T(8,128)(2,1)S(1)}, bf16[1152,128]{1,0:T(8,128)(2,1)S(1)}, u32[]{:S(2)}, u32[]{:S(2)}) collective-permute-start(bf16[1152,128]{1,0:T(8,128)(2,1)S(1)} %copy-done.10), channel_id=1, source_target_pairs={{0,1},{1,2},{2,3},{3,0},{128,131},{129,128},{130,129},{131,130},{4... | collective-permute-start | bytes 884744 | tf_op jit(solution)/shard_map/ppermute | solution.py:459
  115.8 9.3 %collective-permute-start.18 = (bf16[1152,128]{1,0:T(8,128)(2,1)S(1)}, bf16[1152,128]{1,0:T(8,128)(2,1)S(1)}, u32[]{:S(2)}, u32[]{:S(2)}) collective-permute-start(bf16[1152,128]{1,0:T(8,128)(2,1)S(1)} %collective-permute-done.9.refs_1_), channel_id=1, source_target_pairs={{0,1},{1,2},{2,3},{3,0},{128,131},{129,128},{130,129},{131,130},{4... | collective-permute-start | bytes 884744 | tf_op jit(solution)/shard_map/ppermute | solution.py:459
  127.5 10.8 %collective-permute-start.19 = (bf16[8,64,512]{2,1,0:T(8,128)(2,1)}, bf16[8,64,512]{2,1,0:T(8,128)(2,1)S(1)}, u32[]{:S(2)}, u32[]{:S(2)}) collective-permute-start(bf16[8,64,512]{2,1,0:T(8,128)(2,1)} %get-tuple-element.46), channel_id=1, source_target_pairs={{0,128},{128,0},{1,129},{129,1},{2,130},{130,2},{3,131},{131,3},{4... | collective-permute-start | bytes 1572872 | tf_op jit(solution)/shard_map/ppermute | solution.py:570
  130.2 8.2 %collective-permute-start.20 = (bf16[8,4096]{1,0:T(8,128)(2,1)}, bf16[8,4096]{1,0:T(8,128)(2,1)S(1)}, u32[]{:S(2)}, u32[]{:S(2)}) collective-permute-start(bf16[8,4096]{1,0:T(8,128)(2,1)} %get-tuple-element.47), channel_id=1, source_target_pairs={{0,128},{128,0},{1,129},{129,1},{2,130},{130,2},{3,131},{131,3},{4... | collective-permute-start | bytes 196616 | tf_op jit(solution)/shard_map/ppermute | solution.py:570
  (24 other events, 288.1 us)

commit v2 on v1

--- a/solution.py
+++ b/solution.py
@@ -512,10 +512,11 @@
     shares = split(here, q_nope[0], q_rope[0], count)
     hop = turned(shares[2], "hd", 1)
     queries = [shares[0], shifted(shares[1], "hd", 1), None, shifted(shares[3], "hd", 3)]
-    chunk = after(chunk, parts, hop, queries[1], queries[3])
+    chunk = after(chunk, parts, hop)
     queries[2] = turned(hop, "hd", 1)
     near, back = turned(chunk, "y", 1), turned(chunk, "y", -1)
-    far = turned(near, "y", 1)
+    parts = lax.all_to_all(parts, CTX, split_axis=0, concat_axis=0, tiled=True)
+    far = turned(after(near, back, queries[2], parts), "y", 1)
 
     order = (me - jnp.arange(query_blocks, dtype=jnp.int32)) % count
     q = absorb(order, queries, w_uk)
@@ -541,9 +542,8 @@
     codes = turn * (y - wanted // row) % ys * row + wanted % row
     codes = jnp.where(wanted < 0, -1, codes)
 
-    parts = lax.all_to_all(parts, CTX, split_axis=0, concat_axis=0, tiled=True)
+    codes = after(codes, q)
     dec_out = combine(parts, w_uv.shape[0] * VDIM)
-    codes = after(codes, q, dec_out)
     sets = select(codes, (chunk, near, far, back), tuple(layout))
 
     rings, mixtures = [], []
@@ -553,19 +553,24 @@
         at = (first_block + index).reshape(1)
         mixtures.append(attend(index, rings[index], ids, at, ring, q))
 
-    near_sets = []
-    for index, block in enumerate(sets):
-        if index >= 2:
-            block = after(block, *near_sets[index - 2])
-        near_sets.append((turned(block, "hd", 1), turned(block, "hd", -1)))
-    for index, block in enumerate(sets):
+    def neighbours(block):
+        return turned(block, "hd", 1), turned(block, "hd", -1)
+
+    def close(index, *earlier):
         ahead, behind = near_sets[index]
-        earlier = [rings[-1][2], mixtures[-1]] if index >= 2 else []
         far = turned(after(ahead, behind, *earlier), "hd", 1)
-        rings.append((block, ahead, far, behind))
-        if index in (1, 2):
-            mix(index - 1, *near_sets[1])
-    mix(2, mixtures[-1], *near_sets[3])
+        rings.append((sets[index], ahead, far, behind))
+
+    near_sets = [neighbours(sets[0]), neighbours(sets[1])]
+    close(0)
+    close(1)
+    near_sets.append(neighbours(after(sets[2], *near_sets[1])))
+    near_sets.append(neighbours(after(sets[3], *near_sets[1], rings[0][2])))
+    mix(0, *near_sets[1], dec_out)
+    close(2, mixtures[0])
+    mix(1)
+    close(3, mixtures[1])
+    mix(2, mixtures[1], *near_sets[3])
     landed = land(after(ring, mixtures[-1], rings[-1][2]), rings[carrier], slot_count)
     landed_latent, landed_rope = (lax.ppermute(x, "grp", [(0, 1), (1, 0)]) for x in landed)
     last = query_blocks - 1

time: 140 us -> 134 us (0.957)
  waiting for transfers between devices: 26.6 us -> 20.7 us
    ppermute x17, waiting for transfers between devices: 20.7 us -> 9.77 us  [turned(): return lax.ppermute(block, ('grp', axis), route)]
    all_to_all x1, waiting for transfers between devices: 0.25 us -> 8.19 us  [body(): parts = lax.all_to_all(parts, CTX, split_axis=0, concat_axis=0, tiled=True)]
    ppermute x2, waiting for transfers between devices: 5.7 us -> 0.01 us  [shifted(): lax.ppermute(block, axis, [(i, (i + distance) % count) for i in range(cou...]
    all_to_all x1, waiting for transfers between devices: 0.01 us -> 2.75 us  [body(): lax.all_to_all(chunk, ('z', 'hd'), split_axis=0, concat_axis=0, tiled=True)]
    ppermute x17, starting transfers between devices: 28.2 us -> 25.6 us  [turned(): return lax.ppermute(block, ('grp', axis), route)]
    ppermute x2, starting transfers between devices: 2.68 us -> 4.23 us  [body(): lax.ppermute(x, 'grp', [(0, 1), (1, 0)])]
    unnamed x52 -> x50, local copies, waits for them, and re-layouts: 4.48 us -> 4.68 us
  transfers between devices with their start and end apart: 23 -> 23, of which waited for: 10 -> 8; matrix products, arithmetic and copies ran while one was open for 4% -> 5% of each run, Pallas kernels for 31% -> 32%
where the time goes in v2:
time: 134 us
  starting transfers between devices  50.9 us (38%)
  Pallas kernels  50.6 us (38%)
  waiting for transfers between devices  20.7 us (15%)
  local copies, waits for them, and re-layouts  8.39 us (6%)
  other arithmetic  2.37 us (2%)
    pallas_call x4, Pallas kernels, attend(): pl.pallas_call(functools.partial(attend_kernel, len(mixtures)), out_shape...  25.8 us
    ppermute x17, starting transfers between devices, turned(): return lax.ppermute(block, ('grp', axis), route)  25.6 us
    all_to_all x1, starting transfers between devices, body(): lax.all_to_all(chunk, ('z', 'hd'), split_axis=0, concat_axis=0, tiled=True)  11.9 us
    ppermute x17, waiting for transfers between devices, turned(): return lax.ppermute(block, ('grp', axis), route)  9.77 us
    all_to_all x1, waiting for transfers between devices, body(): parts = lax.all_to_all(parts, CTX, split_axis=0, concat_axis=0, tiled=True)  8.19 us
    pallas_call x1, Pallas kernels, decode(): pl.pallas_call(decode_kernel, out_shape=out, grid=(1,), in_specs=[SMALL]...  7.11 us
    all_to_all x1, starting transfers between devices, body(): parts = lax.all_to_all(parts, CTX, split_axis=0, concat_axis=0, tiled=True)  6.48 us
    pallas_call x1, Pallas kernels, absorb(): pl.pallas_call(absorb_kernel, out_shape=jax.ShapeDtypeStruct((blocks, hea...  5.86 us
  transfers between devices with their start and end apart: 23, of which 8 were waited for; matrix products, arithmetic and copies ran while one was open for 5% of the time, Pallas kernels for 32%

profile of v2, /device:TPU:1, one launch (start us, length us, event | category | flops | bytes accessed | tf_op | source)
XLA Modules:
  0.0 133.8 jit_solution(12027042930164061327)
XLA Ops:
  2.6 11.9 %all-to-all-start = ((bf16[32,72,128]{2,1,0:T(8,128)(2,1)}), bf16[32,72,128]{2,1,0:T(8,128)(2,1)S(1)}, u32[]{:S(2)}, u32[]{:S(2)}) async-start(bf16[32,72,128]{2,1,0:T(8,128)(2,1)} %slices.1), calls=%async_computation | async-start | bytes 1179648 | tf_op jit(solution)/shard_map/all_to_all | solution.py:495
  14.5 2.6 %split.1 = (bf16[64,3072]{1,0:T(8,128)(2,1)}, bf16[64,3072]{1,0:T(8,128)(2,1)}, bf16[64,3072]{1,0:T(8,128)(2,1)}, bf16[64,3072]{1,0:T(8,128)(2,1)}) custom-call(s32[1]{0:T(128)} %bitcast.1.me_ref, bf16[64,8192]{1,0:T(8,128)(2,1)} %bitcast.24, bf16[64,4096]{1,0:T(8,128)(2,1)} %bitcast.26), custom_call_target="tpu_custom_call" | custom-call | bytes 3145728 | tf_op jit(solution)/shard_map/split/pallas_call | solution.py:178
  17.1 2.4 %collective-permute-start.1 = (bf16[64,3072]{1,0:T(8,128)(2,1)}, bf16[64,3072]{1,0:T(8,128)(2,1)}, u32[]{:S(2)}, u32[]{:S(2)}) collective-permute-start(bf16[64,3072]{1,0:T(8,128)(2,1)} %get-tuple-element.28), channel_id=1, source_target_pairs={{0,1},{1,2},{2,3},{3,0},{128,131},{129,128},{130,129},{131,130},{4... | collective-permute-start | bytes 1179656 | tf_op jit(solution)/shard_map/ppermute | solution.py:459
  20.3 7.1 %decode.1 = bf16[64,2176]{1,0:T(8,128)(2,1)} custom-call(s32[4,16]{1,0:T(4,128)} %bitcast.34, s32[4]{0:T(128)} %bitcast.35, s32[1]{0:T(128)} %bitcast.11.first_ref.block_ref, bf16[64,2048]{1,0:T(8,128)(2,1)} %bitcast.28, bf16[64,1024]{1,0:T(8,128)(2,1)} %bitcast.29, bf16[16,128,512]{2,1,0:T(8,128)(2,1)} %wuk_ref.1, bf16[16,512,128]{2,1,0:T(8,128)(2,1)} %refs_8_.3, ...), custom_call_target="tpu_custom_call" | custom-call | flops 1000000000 | bytes 7340032 | tf_op jit(solution)/shard_map/decode/pallas_call | solution.py:396
  29.2 2.8 %all-to-all-done.own_ref = bf16[32,72,128]{2,1,0:T(8,128)(2,1)S(1)} async-done(((bf16[32,72,128]{2,1,0:T(8,128)(2,1)}), bf16[32,72,128]{2,1,0:T(8,128)(2,1)S(1)}, u32[]{:S(2)}, u32[]{:S(2)}) %all-to-all-start) | async-done | bytes 589856 | tf_op jit(solution)/shard_map/all_to_all | solution.py:495
  32.0 2.7 %collective-permute-start.4 = (bf16[32,72,128]{2,1,0:T(8,128)(2,1)S(1)}, bf16[32,72,128]{2,1,0:T(8,128)(2,1)S(1)}, u32[]{:S(2)}, u32[]{:S(2)}) collective-permute-start(bf16[32,72,128]{2,1,0:T(8,128)(2,1)S(1)} %all-to-all-done.own_ref), channel_id=1, source_target_pairs={{0,32},{32,64},{64,96},{96,0},{128,224},{160,128},{192,160},{224,1... | collective-permute-start | bytes 1769480 | tf_op jit(solution)/shard_map/ppermute | solution.py:459
  34.7 6.5 %all-to-all-start.1 = ((bf16[32,2,2176]{2,1,0:T(2,128)(2,1)}), bf16[32,2,2176]{2,1,0:T(2,128)(2,1)S(1)}, u32[]{:S(2)}, u32[]{:S(2)}) async-start(bf16[32,2,2176]{2,1,0:T(2,128)(2,1)} %reshape.96), calls=%async_computation.1 | async-start | bytes 557056 | tf_op jit(solution)/shard_map/all_to_all | solution.py:518
  42.9 2.7 %collective-permute-start.3 = (bf16[64,3072]{1,0:T(8,128)(2,1)}, bf16[64,3072]{1,0:T(8,128)(2,1)S(1)}, u32[]{:S(2)}, u32[]{:S(2)}) collective-permute-start(bf16[64,3072]{1,0:T(8,128)(2,1)} %get-tuple-element.29), channel_id=1, source_target_pairs={{0,3},{1,0},{2,1},{3,2},{4,7},{5,4},{6,5},{7,6},{8,11},{9,8},{10,9... | collective-permute-start | bytes 1179656 | tf_op jit(solution)/shard_map/ppermute | solution.py:449
  45.6 8.2 %all-to-all-done.1.parts_ref = bf16[32,2,2176]{2,1,0:T(2,128)(2,1)S(1)} async-done(((bf16[32,2,2176]{2,1,0:T(2,128)(2,1)}), bf16[32,2,2176]{2,1,0:T(2,128)(2,1)S(1)}, u32[]{:S(2)}, u32[]{:S(2)}) %all-to-all-start.1) | async-done | bytes 278560 | tf_op jit(solution)/shard_map/all_to_all | solution.py:518
  57.8 5.9 %absorb.1.refs_4_ = bf16[4,1024,640]{2,1,0:T(8,128)(2,1)} custom-call(s32[4]{0:T(128)} %and_select_fusion.order_ref, bf16[64,3072]{1,0:T(8,128)(2,1)} %get-tuple-element.26.refs_0_.refs_4_, bf16[64,3072]{1,0:T(8,128)(2,1)} %copy-done.2, bf16[64,3072]{1,0:T(8,128)(2,1)} %copy-done.1, bf16[64,3072]{1,0:T(8,128)(2,1)} %copy-done.3, ...), custom_call_target="tpu_custom_call" | custom-call | flops 536870912 | bytes 8912896 | tf_op jit(solution)/shard_map/absorb/pallas_call | solution.py:221
  63.7 2.9 %select.11 = (bf16[1152,128]{1,0:T(8,128)(2,1)}, bf16[1152,128]{1,0:T(8,128)(2,1)}, bf16[1728,128]{1,0:T(8,128)(2,1)}, bf16[1152,128]{1,0:T(8,128)(2,1)}) custom-call(s32[72]{0:T(128)} %fusion.2.code_ref, bf16[32,72,128]{2,1,0:T(8,128)(2,1)} %copy-done, bf16[32,72,128]{2,1,0:T(8,128)(2,1)} %copy-done.5, bf16[32,72,128]{2,1,0:T(8,128)(2,1)} %collective-permute-done.6.far_ref, ...), custom_call_target="tpu_custom_call" | custom-call | tf_op jit(solution)/shard_map/select/pallas_call | solution.py:109
  70.8 2.8 %collective-permute-done.10.refs_3_ = bf16[1152,128]{1,0:T(8,128)(2,1)S(1)} collective-permute-done((bf16[1152,128]{1,0:T(8,128)(2,1)}, bf16[1152,128]{1,0:T(8,128)(2,1)S(1)}, u32[]{:S(2)}, u32[]{:S(2)}) %collective-permute-start.10) | collective-permute-done | bytes 294944 | tf_op jit(solution)/shard_map/ppermute | solution.py:459
  74.4 3.3 %collective-permute-start.11 = (bf16[1152,128]{1,0:T(8,128)(2,1)S(1)}, bf16[1152,128]{1,0:T(8,128)(2,1)S(1)}, u32[]{:S(2)}, u32[]{:S(2)}) collective-permute-start(bf16[1152,128]{1,0:T(8,128)(2,1)S(1)} %collective-permute-done.9.refs_1_), channel_id=1, source_target_pairs={{0,1},{1,2},{2,3},{3,0},{128,131},{129,128},{130,129},{131,130},{4... | collective-permute-start | bytes 884744 | tf_op jit(solution)/shard_map/ppermute | solution.py:459
  77.7 3.0 %collective-permute-done.7.refs_1_ = bf16[1152,128]{1,0:T(8,128)(2,1)S(1)} collective-permute-done((bf16[1152,128]{1,0:T(8,128)(2,1)}, bf16[1152,128]{1,0:T(8,128)(2,1)S(1)}, u32[]{:S(2)}, u32[]{:S(2)}) %collective-permute-start.7) | collective-permute-done | bytes 294944 | tf_op jit(solution)/shard_map/ppermute | solution.py:459
  80.7 3.4 %collective-permute-start.16 = (bf16[1728,128]{1,0:T(8,128)(2,1)}, bf16[1728,128]{1,0:T(8,128)(2,1)S(1)}, u32[]{:S(2)}, u32[]{:S(2)}) collective-permute-start(bf16[1728,128]{1,0:T(8,128)(2,1)} %get-tuple-element.43.refs_0_), channel_id=1, source_target_pairs={{0,1},{1,2},{2,3},{3,0},{128,131},{129,128},{130,129},{131,130},{4... | collective-permute-start | bytes 1327112 | tf_op jit(solution)/shard_map/ppermute | solution.py:459
  84.8 2.0 %combine.1 = bf16[2,2048]{1,0:T(2,128)(2,1)} custom-call(bf16[32,2,2176]{2,1,0:T(2,128)(2,1)} %copy-done.4), custom_call_target="tpu_custom_call" | custom-call | tf_op jit(solution)/shard_map/combine/pallas_call | solution.py:436
  86.8 2.7 %collective-permute-start.14 = (bf16[1152,128]{1,0:T(8,128)(2,1)S(1)}, bf16[1152,128]{1,0:T(8,128)(2,1)S(1)}, u32[]{:S(2)}, u32[]{:S(2)}) collective-permute-start(bf16[1152,128]{1,0:T(8,128)(2,1)S(1)} %collective-permute-done.7.refs_1_), channel_id=1, source_target_pairs={{0,1},{1,2},{2,3},{3,0},{128,131},{129,128},{130,129},{131,130},{4... | collective-permute-start | bytes 884744 | tf_op jit(solution)/shard_map/ppermute | solution.py:459
  90.2 5.9 %attend.5.refs_5_ = bf16[1024,512]{1,0:T(8,128)(2,1)} custom-call(s32[16]{0:T(128)} %get-tuple-element.40.ids_ref, s32[1]{0:T(128)} %bitcast.11.first_ref.block_ref, s32[2]{0:T(128)} %pad_add_fusion.me_ref, bf16[1152,128]{1,0:T(8,128)(2,1)} %get-tuple-element.35.refs_0_, bf16[1152,128]{1,0:T(8,128)(2,1)} %copy-done.21, bf16[1152,128]{1,0:T(8,128)(2,1)} %copy-done.23, ...), custom_call_target="tpu_custom_call" | custom-call | flops 2415919104 | bytes 3538944 | tf_op jit(solution)/shard_map/attend/pallas_call | solution.py:306
  99.7 5.9 %attend.4.refs_6_ = bf16[1024,512]{1,0:T(8,128)(2,1)} custom-call(s32[16]{0:T(128)} %get-tuple-element.50.ids_ref, s32[1]{0:T(128)} %bitcast.15.block_ref, s32[2]{0:T(128)} %pad_add_fusion.me_ref, bf16[1152,128]{1,0:T(8,128)(2,1)} %get-tuple-element.34.refs_0_, bf16[1152,128]{1,0:T(8,128)(2,1)} %copy-done.18, bf16[1152,128]{1,0:T(8,128)(2,1)} %copy-done.22, ...), custom_call_target="tpu_custom_call" | custom-call | flops 2415919104 | bytes 3538944 | tf_op jit(solution)/shard_map/attend/pallas_call | solution.py:306
  107.4 3.5 %collective-permute-start.15 = (bf16[1152,128]{1,0:T(8,128)(2,1)S(1)}, bf16[1152,128]{1,0:T(8,128)(2,1)S(1)}, u32[]{:S(2)}, u32[]{:S(2)}) collective-permute-start(bf16[1152,128]{1,0:T(8,128)(2,1)S(1)} %collective-permute-done.12.refs_1_), channel_id=1, source_target_pairs={{0,1},{1,2},{2,3},{3,0},{128,131},{129,128},{130,129},{131,130},{4... | collective-permute-start | bytes 884744 | tf_op jit(solution)/shard_map/ppermute | solution.py:459
  111.7 5.9 %attend.6.refs_7_ = bf16[1024,512]{1,0:T(8,128)(2,1)} custom-call(s32[16]{0:T(128)} %get-tuple-element.41.ids_ref, s32[1]{0:T(128)} %bitcast.16.block_ref, s32[2]{0:T(128)} %pad_add_fusion.me_ref, bf16[1728,128]{1,0:T(8,128)(2,1)} %get-tuple-element.43.refs_0_, bf16[1728,128]{1,0:T(8,128)(2,1)} %copy-done.7, bf16[1728,128]{1,0:T(8,128)(2,1)} %copy-done.9, ...), custom_call_target="tpu_custom_call" | custom-call | flops 2415919104 | bytes 3538944 | tf_op jit(solution)/shard_map/attend/pallas_call | solution.py:306
  117.6 2.4 %land.1 = (bf16[8,64,512]{2,1,0:T(8,128)(2,1)}, bf16[8,4096]{1,0:T(8,128)(2,1)}) custom-call(s32[2]{0:T(128)} %pad_add_fusion.me_ref, bf16[1728,128]{1,0:T(8,128)(2,1)} %get-tuple-element.43.refs_0_, bf16[1728,128]{1,0:T(8,128)(2,1)} %copy-done.7, bf16[1728,128]{1,0:T(8,128)(2,1)} %copy-done.9, bf16[1728,128]{1,0:T(8,128)(2,1)} %copy-done.8), custom_call_target="tpu_custom_call" | custom-call | tf_op jit(solution)/shard_map/land/pallas_call | solution.py:155
  120.0 4.2 %collective-permute-start.19 = (bf16[8,64,512]{2,1,0:T(8,128)(2,1)}, bf16[8,64,512]{2,1,0:T(8,128)(2,1)S(1)}, u32[]{:S(2)}, u32[]{:S(2)}) collective-permute-start(bf16[8,64,512]{2,1,0:T(8,128)(2,1)} %get-tuple-element.46), channel_id=1, source_target_pairs={{0,128},{128,0},{1,129},{129,1},{2,130},{130,2},{3,131},{131,3},{4... | collective-permute-start | bytes 1572872 | tf_op jit(solution)/shard_map/ppermute | solution.py:575
  124.2 8.1 %attend.7 = bf16[256,2048]{1,0:T(8,128)(2,1)} custom-call(s32[16]{0:T(128)} %copy-done.16, s32[1]{0:T(128)} %bitcast.block_ref, s32[2]{0:T(128)} %pad_add_fusion.me_ref, bf16[1152,128]{1,0:T(8,128)(2,1)} %get-tuple-element.37.refs_0_, bf16[1152,128]{1,0:T(8,128)(2,1)} %copy-done.11, bf16[1152,128]{1,0:T(8,128)(2,1)} %copy-done.13, ...), custom_call_target="tpu_custom_call" | custom-call | flops 2415919104 | bytes 3538944 | tf_op jit(solution)/shard_map/attend/pallas_call | solution.py:306
  (97 shorter events, 24.3 us)
Async XLA Ops:
  2.6 29.4 %all-to-all-start = ((bf16[32,72,128]{2,1,0:T(8,128)(2,1)}), bf16[32,72,128]{2,1,0:T(8,128)(2,1)S(1)}, u32[]{:S(2)}, u32[]{:S(2)}) async-start(bf16[32,72,128]{2,1,0:T(8,128)(2,1)} %slices.1), calls=%async_computation | async-start | bytes 1179648 | tf_op jit(solution)/shard_map/all_to_all | solution.py:495
  17.1 12.1 %collective-permute-start.1 = (bf16[64,3072]{1,0:T(8,128)(2,1)}, bf16[64,3072]{1,0:T(8,128)(2,1)}, u32[]{:S(2)}, u32[]{:S(2)}) collective-permute-start(bf16[64,3072]{1,0:T(8,128)(2,1)} %get-tuple-element.28), channel_id=1, source_target_pairs={{0,1},{1,2},{2,3},{3,0},{128,131},{129,128},{130,129},{131,130},{4... | collective-permute-start | bytes 1179656 | tf_op jit(solution)/shard_map/ppermute | solution.py:459
  20.3 33.6 %copy-start.14 = (s32[1,128,16]{1,2,0:T(8,128)S(1)}, s32[1,128,16]{1,2,0:T(8,128)}, u32[]{:S(2)}) copy-start(s32[1,128,16]{1,2,0:T(8,128)} %param.18) | copy-start | bytes 24580
  32.0 21.9 %collective-permute-start.4 = (bf16[32,72,128]{2,1,0:T(8,128)(2,1)S(1)}, bf16[32,72,128]{2,1,0:T(8,128)(2,1)S(1)}, u32[]{:S(2)}, u32[]{:S(2)}) collective-permute-start(bf16[32,72,128]{2,1,0:T(8,128)(2,1)S(1)} %all-to-all-done.own_ref), channel_id=1, source_target_pairs={{0,32},{32,64},{64,96},{96,0},{128,224},{160,128},{192,160},{224,1... | collective-permute-start | bytes 1769480 | tf_op jit(solution)/shard_map/ppermute | solution.py:459
  34.7 19.1 %collective-permute-start.5 = (bf16[32,72,128]{2,1,0:T(8,128)(2,1)S(1)}, bf16[32,72,128]{2,1,0:T(8,128)(2,1)S(1)}, u32[]{:S(2)}, u32[]{:S(2)}) collective-permute-start(bf16[32,72,128]{2,1,0:T(8,128)(2,1)S(1)} %all-to-all-done.own_ref), channel_id=1, source_target_pairs={{0,96},{32,0},{64,32},{96,64},{128,160},{160,192},{192,224},{224,1... | collective-permute-start | bytes 1769480 | tf_op jit(solution)/shard_map/ppermute | solution.py:459
  34.7 19.1 %all-to-all-start.1 = ((bf16[32,2,2176]{2,1,0:T(2,128)(2,1)}), bf16[32,2,2176]{2,1,0:T(2,128)(2,1)S(1)}, u32[]{:S(2)}, u32[]{:S(2)}) async-start(bf16[32,2,2176]{2,1,0:T(2,128)(2,1)} %reshape.96), calls=%async_computation.1 | async-start | bytes 557056 | tf_op jit(solution)/shard_map/all_to_all | solution.py:518
  41.2 12.6 %collective-permute-start.2 = (bf16[64,3072]{1,0:T(8,128)(2,1)}, bf16[64,3072]{1,0:T(8,128)(2,1)S(1)}, u32[]{:S(2)}, u32[]{:S(2)}) collective-permute-start(bf16[64,3072]{1,0:T(8,128)(2,1)} %collective-permute-done.1), channel_id=1, source_target_pairs={{0,1},{1,2},{2,3},{3,0},{128,131},{129,128},{130,129},{131,130},{4... | collective-permute-start | bytes 1179656 | tf_op jit(solution)/shard_map/ppermute | solution.py:459
  42.9 13.9 %collective-permute-start = (bf16[64,3072]{1,0:T(8,128)(2,1)}, bf16[64,3072]{1,0:T(8,128)(2,1)S(1)}, u32[]{:S(2)}, u32[]{:S(2)}) collective-permute-start(bf16[64,3072]{1,0:T(8,128)(2,1)} %get-tuple-element.27), channel_id=1, source_target_pairs={{0,1},{1,2},{2,3},{3,0},{4,5},{5,6},{6,7},{7,4},{8,9},{9,10},{10,1... | collective-permute-start | bytes 1179656 | tf_op jit(solution)/shard_map/ppermute | solution.py:449
  42.9 13.9 %collective-permute-start.3 = (bf16[64,3072]{1,0:T(8,128)(2,1)}, bf16[64,3072]{1,0:T(8,128)(2,1)S(1)}, u32[]{:S(2)}, u32[]{:S(2)}) collective-permute-start(bf16[64,3072]{1,0:T(8,128)(2,1)} %get-tuple-element.29), channel_id=1, source_target_pairs={{0,3},{1,0},{2,1},{3,2},{4,7},{5,4},{6,5},{7,6},{8,11},{9,8},{10,9... | collective-permute-start | bytes 1179656 | tf_op jit(solution)/shard_map/ppermute | solution.py:449
  53.9 9.8 %collective-permute-start.6 = (bf16[32,72,128]{2,1,0:T(8,128)(2,1)S(1)}, bf16[32,72,128]{2,1,0:T(8,128)(2,1)}, u32[]{:S(2)}, u32[]{:S(2)}) collective-permute-start(bf16[32,72,128]{2,1,0:T(8,128)(2,1)S(1)} %collective-permute-done.4.near_ref), channel_id=1, source_target_pairs={{0,32},{32,64},{64,96},{96,0},{128,224},{160,128},{192,160},{224,1... | collective-permute-start | bytes 1769480 | tf_op jit(solution)/shard_map/ppermute | solution.py:459
  66.6 7.0 %collective-permute-start.10 = (bf16[1152,128]{1,0:T(8,128)(2,1)}, bf16[1152,128]{1,0:T(8,128)(2,1)S(1)}, u32[]{:S(2)}, u32[]{:S(2)}) collective-permute-start(bf16[1152,128]{1,0:T(8,128)(2,1)} %get-tuple-element.35.refs_0_), channel_id=1, source_target_pairs={{0,3},{1,0},{2,1},{3,2},{128,129},{129,130},{130,131},{131,128},{4... | collective-permute-start | bytes 884744 | tf_op jit(solution)/shard_map/ppermute | solution.py:459
  67.8 6.6 %collective-permute-start.9 = (bf16[1152,128]{1,0:T(8,128)(2,1)}, bf16[1152,128]{1,0:T(8,128)(2,1)S(1)}, u32[]{:S(2)}, u32[]{:S(2)}) collective-permute-start(bf16[1152,128]{1,0:T(8,128)(2,1)} %get-tuple-element.35.refs_0_), channel_id=1, source_target_pairs={{0,1},{1,2},{2,3},{3,0},{128,131},{129,128},{130,129},{131,130},{4... | collective-permute-start | bytes 884744 | tf_op jit(solution)/shard_map/ppermute | solution.py:459
  69.3 11.4 %collective-permute-start.7 = (bf16[1152,128]{1,0:T(8,128)(2,1)}, bf16[1152,128]{1,0:T(8,128)(2,1)S(1)}, u32[]{:S(2)}, u32[]{:S(2)}) collective-permute-start(bf16[1152,128]{1,0:T(8,128)(2,1)} %get-tuple-element.34.refs_0_), channel_id=1, source_target_pairs={{0,1},{1,2},{2,3},{3,0},{128,131},{129,128},{130,129},{131,130},{4... | collective-permute-start | bytes 884744 | tf_op jit(solution)/shard_map/ppermute | solution.py:459
  70.6 10.1 %collective-permute-start.8 = (bf16[1152,128]{1,0:T(8,128)(2,1)}, bf16[1152,128]{1,0:T(8,128)(2,1)S(1)}, u32[]{:S(2)}, u32[]{:S(2)}) collective-permute-start(bf16[1152,128]{1,0:T(8,128)(2,1)} %get-tuple-element.34.refs_0_), channel_id=1, source_target_pairs={{0,3},{1,0},{2,1},{3,2},{128,129},{129,130},{130,131},{131,128},{4... | collective-permute-start | bytes 884744 | tf_op jit(solution)/shard_map/ppermute | solution.py:459
  74.4 15.1 %collective-permute-start.11 = (bf16[1152,128]{1,0:T(8,128)(2,1)S(1)}, bf16[1152,128]{1,0:T(8,128)(2,1)S(1)}, u32[]{:S(2)}, u32[]{:S(2)}) collective-permute-start(bf16[1152,128]{1,0:T(8,128)(2,1)S(1)} %collective-permute-done.9.refs_1_), channel_id=1, source_target_pairs={{0,1},{1,2},{2,3},{3,0},{128,131},{129,128},{130,129},{131,130},{4... | collective-permute-start | bytes 884744 | tf_op jit(solution)/shard_map/ppermute | solution.py:459
  80.7 15.4 %collective-permute-start.16 = (bf16[1728,128]{1,0:T(8,128)(2,1)}, bf16[1728,128]{1,0:T(8,128)(2,1)S(1)}, u32[]{:S(2)}, u32[]{:S(2)}) collective-permute-start(bf16[1728,128]{1,0:T(8,128)(2,1)} %get-tuple-element.43.refs_0_), channel_id=1, source_target_pairs={{0,1},{1,2},{2,3},{3,0},{128,131},{129,128},{130,129},{131,130},{4... | collective-permute-start | bytes 1327112 | tf_op jit(solution)/shard_map/ppermute | solution.py:459
  84.1 12.2 %collective-permute-start.17 = (bf16[1728,128]{1,0:T(8,128)(2,1)}, bf16[1728,128]{1,0:T(8,128)(2,1)S(1)}, u32[]{:S(2)}, u32[]{:S(2)}) collective-permute-start(bf16[1728,128]{1,0:T(8,128)(2,1)} %get-tuple-element.43.refs_0_), channel_id=1, source_target_pairs={{0,3},{1,0},{2,1},{3,2},{128,129},{129,130},{130,131},{131,128},{4... | collective-permute-start | bytes 1327112 | tf_op jit(solution)/shard_map/ppermute | solution.py:459
  86.8 12.2 %collective-permute-start.14 = (bf16[1152,128]{1,0:T(8,128)(2,1)S(1)}, bf16[1152,128]{1,0:T(8,128)(2,1)S(1)}, u32[]{:S(2)}, u32[]{:S(2)}) collective-permute-start(bf16[1152,128]{1,0:T(8,128)(2,1)S(1)} %collective-permute-done.7.refs_1_), channel_id=1, source_target_pairs={{0,1},{1,2},{2,3},{3,0},{128,131},{129,128},{130,129},{131,130},{4... | collective-permute-start | bytes 884744 | tf_op jit(solution)/shard_map/ppermute | solution.py:459
  96.3 14.6 %collective-permute-start.18 = (bf16[1728,128]{1,0:T(8,128)(2,1)S(1)}, bf16[1728,128]{1,0:T(8,128)(2,1)S(1)}, u32[]{:S(2)}, u32[]{:S(2)}) collective-permute-start(bf16[1728,128]{1,0:T(8,128)(2,1)S(1)} %collective-permute-done.16.refs_1_), channel_id=1, source_target_pairs={{0,1},{1,2},{2,3},{3,0},{128,131},{129,128},{130,129},{131,130},{4... | collective-permute-start | bytes 1327112 | tf_op jit(solution)/shard_map/ppermute | solution.py:459
  96.3 11.1 %collective-permute-start.12 = (bf16[1152,128]{1,0:T(8,128)(2,1)S(1)}, bf16[1152,128]{1,0:T(8,128)(2,1)S(1)}, u32[]{:S(2)}, u32[]{:S(2)}) collective-permute-start(bf16[1152,128]{1,0:T(8,128)(2,1)S(1)} %copy-done.10), channel_id=1, source_target_pairs={{0,1},{1,2},{2,3},{3,0},{128,131},{129,128},{130,129},{131,130},{4... | collective-permute-start | bytes 884744 | tf_op jit(solution)/shard_map/ppermute | solution.py:459
  96.5 10.9 %collective-permute-start.13 = (bf16[1152,128]{1,0:T(8,128)(2,1)S(1)}, bf16[1152,128]{1,0:T(8,128)(2,1)S(1)}, u32[]{:S(2)}, u32[]{:S(2)}) collective-permute-start(bf16[1152,128]{1,0:T(8,128)(2,1)S(1)} %copy-done.10), channel_id=1, source_target_pairs={{0,3},{1,0},{2,1},{3,2},{128,129},{129,130},{130,131},{131,128},{4... | collective-permute-start | bytes 884744 | tf_op jit(solution)/shard_map/ppermute | solution.py:459
  107.4 10.2 %collective-permute-start.15 = (bf16[1152,128]{1,0:T(8,128)(2,1)S(1)}, bf16[1152,128]{1,0:T(8,128)(2,1)S(1)}, u32[]{:S(2)}, u32[]{:S(2)}) collective-permute-start(bf16[1152,128]{1,0:T(8,128)(2,1)S(1)} %collective-permute-done.12.refs_1_), channel_id=1, source_target_pairs={{0,1},{1,2},{2,3},{3,0},{128,131},{129,128},{130,129},{131,130},{4... | collective-permute-start | bytes 884744 | tf_op jit(solution)/shard_map/ppermute | solution.py:459
  120.0 12.4 %collective-permute-start.19 = (bf16[8,64,512]{2,1,0:T(8,128)(2,1)}, bf16[8,64,512]{2,1,0:T(8,128)(2,1)S(1)}, u32[]{:S(2)}, u32[]{:S(2)}) collective-permute-start(bf16[8,64,512]{2,1,0:T(8,128)(2,1)} %get-tuple-element.46), channel_id=1, source_target_pairs={{0,128},{128,0},{1,129},{129,1},{2,130},{130,2},{3,131},{131,3},{4... | collective-permute-start | bytes 1572872 | tf_op jit(solution)/shard_map/ppermute | solution.py:575
  124.2 8.2 %collective-permute-start.20 = (bf16[8,4096]{1,0:T(8,128)(2,1)}, bf16[8,4096]{1,0:T(8,128)(2,1)S(1)}, u32[]{:S(2)}, u32[]{:S(2)}) collective-permute-start(bf16[8,4096]{1,0:T(8,128)(2,1)} %get-tuple-element.47), channel_id=1, source_target_pairs={{0,128},{128,0},{1,129},{129,1},{2,130},{130,2},{3,131},{131,3},{4... | collective-permute-start | bytes 196616 | tf_op jit(solution)/shard_map/ppermute | solution.py:575
  (23 other events, 250.3 us)

commit v3 on v2

--- a/solution.py
+++ b/solution.py
@@ -113,7 +113,7 @@
         in_specs=[SMALL] + [whole(part) for part in gathered],
         out_specs=[whole(out) for out in outs],
         scratch_shapes=[pltpu.VMEM((sources, PART, FEAT), BF16)],
-        compiler_params=PARAMS,
+        compiler_params=pltpu.CompilerParams(vmem_limit_bytes=16 * 1024 * 1024),
         name="select",
     )(codes, *gathered)
 
@@ -232,7 +232,7 @@
             bytes_accessed=rows * (WIDE + 192) * 2 + heads * NOPE * LAT * 2,
             transcendentals=0,
         ),
-        compiler_params=PARAMS,
+        compiler_params=pltpu.CompilerParams(vmem_limit_bytes=24 * 1024 * 1024),
         name="absorb",
     )(order, *queries, *queries, w_uk)
 
@@ -562,11 +562,11 @@
         rings.append((sets[index], ahead, far, behind))
 
     near_sets = [neighbours(sets[0]), neighbours(sets[1])]
-    close(0)
+    close(0, dec_out, ring)
     close(1)
     near_sets.append(neighbours(after(sets[2], *near_sets[1])))
     near_sets.append(neighbours(after(sets[3], *near_sets[1], rings[0][2])))
-    mix(0, *near_sets[1], dec_out)
+    mix(0, *near_sets[1])
     close(2, mixtures[0])
     mix(1)
     close(3, mixtures[1])

time: 134 us -> 133 us (level)
  Pallas kernels: 50.6 us -> 47.2 us
  local copies, waits for them, and re-layouts: 8.39 us -> 10.3 us
    pallas_call x1, Pallas kernels: 5.86 us -> 3.55 us  [absorb(): pl.pallas_call(absorb_kernel, out_shape=jax.ShapeDtypeStruct((blocks, hea...]
  transfers between devices with their start and end apart: 23 -> 23, of which waited for: 8 -> 7; matrix products, arithmetic and copies ran while one was open for 5% -> 6% of each run, Pallas kernels for 32% -> 31%
where the time goes in v3:
time: 133 us
  starting transfers between devices  51.4 us (39%)
  Pallas kernels  47.2 us (35%)
  waiting for transfers between devices  19.6 us (15%)
  local copies, waits for them, and re-layouts  10.3 us (8%)
  other arithmetic  3.18 us (2%)
    ppermute x17, starting transfers between devices, turned(): return lax.ppermute(block, ('grp', axis), route)  26.1 us
    pallas_call x4, Pallas kernels, attend(): pl.pallas_call(functools.partial(attend_kernel, len(mixtures)), out_shape...  25.8 us
    all_to_all x1, starting transfers between devices, body(): lax.all_to_all(chunk, ('z', 'hd'), split_axis=0, concat_axis=0, tiled=True)  11.9 us
    ppermute x17, waiting for transfers between devices, turned(): return lax.ppermute(block, ('grp', axis), route)  9.29 us
    all_to_all x1, waiting for transfers between devices, body(): parts = lax.all_to_all(parts, CTX, split_axis=0, concat_axis=0, tiled=True)  7.65 us
    pallas_call x1, Pallas kernels, decode(): pl.pallas_call(decode_kernel, out_shape=out, grid=(1,), in_specs=[SMALL]...  7.2 us
    all_to_all x1, starting transfers between devices, body(): parts = lax.all_to_all(parts, CTX, split_axis=0, concat_axis=0, tiled=True)  6.71 us
    unnamed x50, local copies, waits for them, and re-layouts  6.01 us
  transfers between devices with their start and end apart: 23, of which 7 were waited for; matrix products, arithmetic and copies ran while one was open for 6% of the time, Pallas kernels for 31%

profile of v3, /device:TPU:1, one launch (start us, length us, event | category | flops | bytes accessed | tf_op | source)
XLA Modules:
  0.0 132.7 jit_solution(10062319201734556080)
XLA Ops:
  2.6 11.9 %all-to-all-start = ((bf16[32,72,128]{2,1,0:T(8,128)(2,1)}), bf16[32,72,128]{2,1,0:T(8,128)(2,1)S(1)}, u32[]{:S(2)}, u32[]{:S(2)}) async-start(bf16[32,72,128]{2,1,0:T(8,128)(2,1)} %slices.1), calls=%async_computation | async-start | bytes 1179648 | tf_op jit(solution)/shard_map/all_to_all | solution.py:495
  14.5 2.6 %split.1 = (bf16[64,3072]{1,0:T(8,128)(2,1)}, bf16[64,3072]{1,0:T(8,128)(2,1)}, bf16[64,3072]{1,0:T(8,128)(2,1)}, bf16[64,3072]{1,0:T(8,128)(2,1)}) custom-call(s32[1]{0:T(128)} %bitcast.1.me_ref, bf16[64,8192]{1,0:T(8,128)(2,1)} %bitcast.24, bf16[64,4096]{1,0:T(8,128)(2,1)} %bitcast.26), custom_call_target="tpu_custom_call" | custom-call | bytes 3145728 | tf_op jit(solution)/shard_map/split/pallas_call | solution.py:178
  17.1 2.4 %collective-permute-start.1 = (bf16[64,3072]{1,0:T(8,128)(2,1)}, bf16[64,3072]{1,0:T(8,128)(2,1)S(1)}, u32[]{:S(2)}, u32[]{:S(2)}) collective-permute-start(bf16[64,3072]{1,0:T(8,128)(2,1)} %get-tuple-element.28), channel_id=1, source_target_pairs={{0,1},{1,2},{2,3},{3,0},{128,131},{129,128},{130,129},{131,130},{4... | collective-permute-start | bytes 1179656 | tf_op jit(solution)/shard_map/ppermute | solution.py:459
  20.4 7.2 %decode.1 = bf16[64,2176]{1,0:T(8,128)(2,1)} custom-call(s32[4,16]{1,0:T(4,128)} %bitcast.34, s32[4]{0:T(128)} %bitcast.35, s32[1]{0:T(128)} %bitcast.11.first_ref.block_ref, bf16[64,2048]{1,0:T(8,128)(2,1)} %bitcast.28, bf16[64,1024]{1,0:T(8,128)(2,1)} %bitcast.29, bf16[16,128,512]{2,1,0:T(8,128)(2,1)} %wuk_ref.1, bf16[16,512,128]{2,1,0:T(8,128)(2,1)} %refs_8_.3, ...), custom_call_target="tpu_custom_call" | custom-call | flops 1000000000 | bytes 7340032 | tf_op jit(solution)/shard_map/decode/pallas_call | solution.py:396
  29.3 2.6 %all-to-all-done.own_ref = bf16[32,72,128]{2,1,0:T(8,128)(2,1)S(1)} async-done(((bf16[32,72,128]{2,1,0:T(8,128)(2,1)}), bf16[32,72,128]{2,1,0:T(8,128)(2,1)S(1)}, u32[]{:S(2)}, u32[]{:S(2)}) %all-to-all-start) | async-done | bytes 589856 | tf_op jit(solution)/shard_map/all_to_all | solution.py:495
  32.0 2.7 %collective-permute-start.4 = (bf16[32,72,128]{2,1,0:T(8,128)(2,1)S(1)}, bf16[32,72,128]{2,1,0:T(8,128)(2,1)}, u32[]{:S(2)}, u32[]{:S(2)}) collective-permute-start(bf16[32,72,128]{2,1,0:T(8,128)(2,1)S(1)} %all-to-all-done.own_ref), channel_id=1, source_target_pairs={{0,32},{32,64},{64,96},{96,0},{128,224},{160,128},{192,160},{224,1... | collective-permute-start | bytes 1769480 | tf_op jit(solution)/shard_map/ppermute | solution.py:459
  34.7 6.7 %all-to-all-start.1 = ((bf16[32,2,2176]{2,1,0:T(2,128)(2,1)}), bf16[32,2,2176]{2,1,0:T(2,128)(2,1)}, u32[]{:S(2)}, u32[]{:S(2)}) async-start(bf16[32,2,2176]{2,1,0:T(2,128)(2,1)} %reshape.96), calls=%async_computation.1 | async-start | bytes 557056 | tf_op jit(solution)/shard_map/all_to_all | solution.py:518
  43.0 2.7 %collective-permute-start.3 = (bf16[64,3072]{1,0:T(8,128)(2,1)}, bf16[64,3072]{1,0:T(8,128)(2,1)}, u32[]{:S(2)}, u32[]{:S(2)}) collective-permute-start(bf16[64,3072]{1,0:T(8,128)(2,1)} %get-tuple-element.29), channel_id=1, source_target_pairs={{0,3},{1,0},{2,1},{3,2},{4,7},{5,4},{6,5},{7,6},{8,11},{9,8},{10,9... | collective-permute-start | bytes 1179656 | tf_op jit(solution)/shard_map/ppermute | solution.py:449
  46.2 7.7 %all-to-all-done.1.parts_ref = bf16[32,2,2176]{2,1,0:T(2,128)(2,1)} async-done(((bf16[32,2,2176]{2,1,0:T(2,128)(2,1)}), bf16[32,2,2176]{2,1,0:T(2,128)(2,1)}, u32[]{:S(2)}, u32[]{:S(2)}) %all-to-all-start.1) | async-done | bytes 278560 | tf_op jit(solution)/shard_map/all_to_all | solution.py:518
  57.8 3.6 %absorb.1.refs_4_ = bf16[4,1024,640]{2,1,0:T(8,128)(2,1)S(1)} custom-call(s32[4]{0:T(128)S(1)} %and_select_fusion.order_ref, bf16[64,3072]{1,0:T(8,128)(2,1)S(1)} %copy-done.2, bf16[64,3072]{1,0:T(8,128)(2,1)} %collective-permute-done.refs_1_.refs_5_, bf16[64,3072]{1,0:T(8,128)(2,1)S(1)} %collective-permute-done.2.refs_2_.refs_6_, ...), custom_call_target="tpu_custom_call" | custom-call | flops 536870912 | bytes 8912896 | tf_op jit(solution)/shard_map/absorb/pallas_call | solution.py:221
  61.4 2.3 %copy-done = bf16[4,1024,640]{2,1,0:T(8,128)(2,1)} copy-done((bf16[4,1024,640]{2,1,0:T(8,128)(2,1)}, bf16[4,1024,640]{2,1,0:T(8,128)(2,1)S(1)}, u32[]{:S(2)}) %copy-start) | copy-done | bytes 5242904
  70.6 2.0 %combine.1 = bf16[2,2048]{1,0:T(2,128)(2,1)} custom-call(bf16[32,2,2176]{2,1,0:T(2,128)(2,1)} %all-to-all-done.1.parts_ref), custom_call_target="tpu_custom_call" | custom-call | tf_op jit(solution)/shard_map/combine/pallas_call | solution.py:436
  73.1 3.4 %collective-permute-start.11 = (bf16[1152,128]{1,0:T(8,128)(2,1)S(1)}, bf16[1152,128]{1,0:T(8,128)(2,1)S(1)}, u32[]{:S(2)}, u32[]{:S(2)}) collective-permute-start(bf16[1152,128]{1,0:T(8,128)(2,1)S(1)} %collective-permute-done.9.refs_1_), channel_id=1, source_target_pairs={{0,1},{1,2},{2,3},{3,0},{128,131},{129,128},{130,129},{131,130},{4... | collective-permute-start | bytes 884744 | tf_op jit(solution)/shard_map/ppermute | solution.py:459
  76.5 2.9 %collective-permute-done.7.refs_1_ = bf16[1152,128]{1,0:T(8,128)(2,1)S(1)} collective-permute-done((bf16[1152,128]{1,0:T(8,128)(2,1)S(1)}, bf16[1152,128]{1,0:T(8,128)(2,1)S(1)}, u32[]{:S(2)}, u32[]{:S(2)}) %collective-permute-start.7) | collective-permute-done | bytes 294944 | tf_op jit(solution)/shard_map/ppermute | solution.py:459
  79.4 3.5 %collective-permute-start.16 = (bf16[1728,128]{1,0:T(8,128)(2,1)S(1)}, bf16[1728,128]{1,0:T(8,128)(2,1)S(1)}, u32[]{:S(2)}, u32[]{:S(2)}) collective-permute-start(bf16[1728,128]{1,0:T(8,128)(2,1)S(1)} %get-tuple-element.43.refs_0_), channel_id=1, source_target_pairs={{0,1},{1,2},{2,3},{3,0},{128,131},{129,128},{130,129},{131,130},{4... | collective-permute-start | bytes 1327112 | tf_op jit(solution)/shard_map/ppermute | solution.py:459
  82.9 2.7 %collective-permute-start.14 = (bf16[1152,128]{1,0:T(8,128)(2,1)S(1)}, bf16[1152,128]{1,0:T(8,128)(2,1)S(1)}, u32[]{:S(2)}, u32[]{:S(2)}) collective-permute-start(bf16[1152,128]{1,0:T(8,128)(2,1)S(1)} %collective-permute-done.7.refs_1_), channel_id=1, source_target_pairs={{0,1},{1,2},{2,3},{3,0},{128,131},{129,128},{130,129},{131,130},{4... | collective-permute-start | bytes 884744 | tf_op jit(solution)/shard_map/ppermute | solution.py:459
  86.3 5.9 %attend.5.refs_5_ = bf16[1024,512]{1,0:T(8,128)(2,1)} custom-call(s32[16]{0:T(128)} %get-tuple-element.40.ids_ref, s32[1]{0:T(128)} %bitcast.11.first_ref.block_ref, s32[2]{0:T(128)} %pad_add_fusion.me_ref, bf16[1152,128]{1,0:T(8,128)(2,1)} %copy-done.6, bf16[1152,128]{1,0:T(8,128)(2,1)} %copy-done.21, bf16[1152,128]{1,0:T(8,128)(2,1)} %copy-done.23, ...), custom_call_target="tpu_custom_call" | custom-call | flops 2415919104 | bytes 3538944 | tf_op jit(solution)/shard_map/attend/pallas_call | solution.py:306
  92.2 2.9 %collective-permute-done.17.refs_3_ = bf16[1728,128]{1,0:T(8,128)(2,1)S(1)} collective-permute-done((bf16[1728,128]{1,0:T(8,128)(2,1)S(1)}, bf16[1728,128]{1,0:T(8,128)(2,1)S(1)}, u32[]{:S(2)}, u32[]{:S(2)}) %collective-permute-start.17) | collective-permute-done | bytes 442400 | tf_op jit(solution)/shard_map/ppermute | solution.py:459
  98.5 5.9 %attend.4.refs_6_ = bf16[1024,512]{1,0:T(8,128)(2,1)} custom-call(s32[16]{0:T(128)} %get-tuple-element.50.ids_ref, s32[1]{0:T(128)} %bitcast.15.block_ref, s32[2]{0:T(128)} %pad_add_fusion.me_ref, bf16[1152,128]{1,0:T(8,128)(2,1)} %copy-done.5, bf16[1152,128]{1,0:T(8,128)(2,1)} %copy-done.18, bf16[1152,128]{1,0:T(8,128)(2,1)} %copy-done.22, ...), custom_call_target="tpu_custom_call" | custom-call | flops 2415919104 | bytes 3538944 | tf_op jit(solution)/shard_map/attend/pallas_call | solution.py:306
  106.2 3.7 %collective-permute-start.15 = (bf16[1152,128]{1,0:T(8,128)(2,1)S(1)}, bf16[1152,128]{1,0:T(8,128)(2,1)S(1)}, u32[]{:S(2)}, u32[]{:S(2)}) collective-permute-start(bf16[1152,128]{1,0:T(8,128)(2,1)S(1)} %collective-permute-done.12.refs_1_), channel_id=1, source_target_pairs={{0,1},{1,2},{2,3},{3,0},{128,131},{129,128},{130,129},{131,130},{4... | collective-permute-start | bytes 884744 | tf_op jit(solution)/shard_map/ppermute | solution.py:459
  110.7 5.9 %attend.6.refs_7_ = bf16[1024,512]{1,0:T(8,128)(2,1)} custom-call(s32[16]{0:T(128)} %get-tuple-element.41.ids_ref, s32[1]{0:T(128)} %bitcast.16.block_ref, s32[2]{0:T(128)} %pad_add_fusion.me_ref, bf16[1728,128]{1,0:T(8,128)(2,1)} %copy-done.3, bf16[1728,128]{1,0:T(8,128)(2,1)} %copy-done.7, bf16[1728,128]{1,0:T(8,128)(2,1)} %copy-done.9, ...), custom_call_target="tpu_custom_call" | custom-call | flops 2415919104 | bytes 3538944 | tf_op jit(solution)/shard_map/attend/pallas_call | solution.py:306
  116.6 2.4 %land.1 = (bf16[8,64,512]{2,1,0:T(8,128)(2,1)}, bf16[8,4096]{1,0:T(8,128)(2,1)}) custom-call(s32[2]{0:T(128)} %pad_add_fusion.me_ref, bf16[1728,128]{1,0:T(8,128)(2,1)} %copy-done.3, bf16[1728,128]{1,0:T(8,128)(2,1)} %copy-done.7, bf16[1728,128]{1,0:T(8,128)(2,1)} %copy-done.9, bf16[1728,128]{1,0:T(8,128)(2,1)} %copy-done.8), custom_call_target="tpu_custom_call" | custom-call | tf_op jit(solution)/shard_map/land/pallas_call | solution.py:155
  119.0 4.1 %collective-permute-start.19 = (bf16[8,64,512]{2,1,0:T(8,128)(2,1)}, bf16[8,64,512]{2,1,0:T(8,128)(2,1)S(1)}, u32[]{:S(2)}, u32[]{:S(2)}) collective-permute-start(bf16[8,64,512]{2,1,0:T(8,128)(2,1)} %get-tuple-element.46), channel_id=1, source_target_pairs={{0,128},{128,0},{1,129},{129,1},{2,130},{130,2},{3,131},{131,3},{4... | collective-permute-start | bytes 1572872 | tf_op jit(solution)/shard_map/ppermute | solution.py:575
  123.1 8.1 %attend.7 = bf16[256,2048]{1,0:T(8,128)(2,1)} custom-call(s32[16]{0:T(128)} %copy-done.15, s32[1]{0:T(128)} %bitcast.block_ref, s32[2]{0:T(128)} %pad_add_fusion.me_ref, bf16[1152,128]{1,0:T(8,128)(2,1)} %copy-done.4, bf16[1152,128]{1,0:T(8,128)(2,1)} %copy-done.10, bf16[1152,128]{1,0:T(8,128)(2,1)} %copy-done.12, bf16[1152,128]{1,0:T(8,128)(2,1)} %copy-done.11, ...), custom_call_target="tpu_custom_call" | custom-call | flops 2415919104 | bytes 3538944 | tf_op jit(solution)/shard_map/attend/pallas_call | solution.py:306
  (97 shorter events, 25.9 us)
Async XLA Ops:
  2.6 29.4 %all-to-all-start = ((bf16[32,72,128]{2,1,0:T(8,128)(2,1)}), bf16[32,72,128]{2,1,0:T(8,128)(2,1)S(1)}, u32[]{:S(2)}, u32[]{:S(2)}) async-start(bf16[32,72,128]{2,1,0:T(8,128)(2,1)} %slices.1), calls=%async_computation | async-start | bytes 1179648 | tf_op jit(solution)/shard_map/all_to_all | solution.py:495
  17.1 12.2 %collective-permute-start.1 = (bf16[64,3072]{1,0:T(8,128)(2,1)}, bf16[64,3072]{1,0:T(8,128)(2,1)S(1)}, u32[]{:S(2)}, u32[]{:S(2)}) collective-permute-start(bf16[64,3072]{1,0:T(8,128)(2,1)} %get-tuple-element.28), channel_id=1, source_target_pairs={{0,1},{1,2},{2,3},{3,0},{128,131},{129,128},{130,129},{131,130},{4... | collective-permute-start | bytes 1179656 | tf_op jit(solution)/shard_map/ppermute | solution.py:459
  20.3 37.4 %copy-start.2 = (bf16[64,3072]{1,0:T(8,128)(2,1)S(1)}, bf16[64,3072]{1,0:T(8,128)(2,1)}, u32[]{:S(2)}) copy-start(bf16[64,3072]{1,0:T(8,128)(2,1)} %get-tuple-element.26.refs_0_.refs_4_) | copy-start | bytes 1179652
  32.0 21.9 %collective-permute-start.4 = (bf16[32,72,128]{2,1,0:T(8,128)(2,1)S(1)}, bf16[32,72,128]{2,1,0:T(8,128)(2,1)}, u32[]{:S(2)}, u32[]{:S(2)}) collective-permute-start(bf16[32,72,128]{2,1,0:T(8,128)(2,1)S(1)} %all-to-all-done.own_ref), channel_id=1, source_target_pairs={{0,32},{32,64},{64,96},{96,0},{128,224},{160,128},{192,160},{224,1... | collective-permute-start | bytes 1769480 | tf_op jit(solution)/shard_map/ppermute | solution.py:459
  34.7 19.2 %collective-permute-start.5 = (bf16[32,72,128]{2,1,0:T(8,128)(2,1)S(1)}, bf16[32,72,128]{2,1,0:T(8,128)(2,1)}, u32[]{:S(2)}, u32[]{:S(2)}) collective-permute-start(bf16[32,72,128]{2,1,0:T(8,128)(2,1)S(1)} %all-to-all-done.own_ref), channel_id=1, source_target_pairs={{0,96},{32,0},{64,32},{96,64},{128,160},{160,192},{192,224},{224,1... | collective-permute-start | bytes 1769480 | tf_op jit(solution)/shard_map/ppermute | solution.py:459
  34.7 19.2 %all-to-all-start.1 = ((bf16[32,2,2176]{2,1,0:T(2,128)(2,1)}), bf16[32,2,2176]{2,1,0:T(2,128)(2,1)}, u32[]{:S(2)}, u32[]{:S(2)}) async-start(bf16[32,2,2176]{2,1,0:T(2,128)(2,1)} %reshape.96), calls=%async_computation.1 | async-start | bytes 557056 | tf_op jit(solution)/shard_map/all_to_all | solution.py:518
  41.4 12.5 %collective-permute-start.2 = (bf16[64,3072]{1,0:T(8,128)(2,1)}, bf16[64,3072]{1,0:T(8,128)(2,1)S(1)}, u32[]{:S(2)}, u32[]{:S(2)}) collective-permute-start(bf16[64,3072]{1,0:T(8,128)(2,1)} %copy-done.17), channel_id=1, source_target_pairs={{0,1},{1,2},{2,3},{3,0},{128,131},{129,128},{130,129},{131,130},{4... | collective-permute-start | bytes 1179656 | tf_op jit(solution)/shard_map/ppermute | solution.py:459
  43.0 14.7 %collective-permute-start = (bf16[64,3072]{1,0:T(8,128)(2,1)}, bf16[64,3072]{1,0:T(8,128)(2,1)}, u32[]{:S(2)}, u32[]{:S(2)}) collective-permute-start(bf16[64,3072]{1,0:T(8,128)(2,1)} %get-tuple-element.27), channel_id=1, source_target_pairs={{0,1},{1,2},{2,3},{3,0},{4,5},{5,6},{6,7},{7,4},{8,9},{9,10},{10,1... | collective-permute-start | bytes 1179656 | tf_op jit(solution)/shard_map/ppermute | solution.py:449
  43.0 14.7 %collective-permute-start.3 = (bf16[64,3072]{1,0:T(8,128)(2,1)}, bf16[64,3072]{1,0:T(8,128)(2,1)}, u32[]{:S(2)}, u32[]{:S(2)}) collective-permute-start(bf16[64,3072]{1,0:T(8,128)(2,1)} %get-tuple-element.29), channel_id=1, source_target_pairs={{0,3},{1,0},{2,1},{3,2},{4,7},{5,4},{6,5},{7,6},{8,11},{9,8},{10,9... | collective-permute-start | bytes 1179656 | tf_op jit(solution)/shard_map/ppermute | solution.py:449
  53.9 9.8 %collective-permute-start.6 = (bf16[32,72,128]{2,1,0:T(8,128)(2,1)}, bf16[32,72,128]{2,1,0:T(8,128)(2,1)}, u32[]{:S(2)}, u32[]{:S(2)}) collective-permute-start(bf16[32,72,128]{2,1,0:T(8,128)(2,1)} %collective-permute-done.4.near_ref), channel_id=1, source_target_pairs={{0,32},{32,64},{64,96},{96,0},{128,224},{160,128},{192,160},{224,1... | collective-permute-start | bytes 1769480 | tf_op jit(solution)/shard_map/ppermute | solution.py:459
  65.5 7.1 %collective-permute-start.10 = (bf16[1152,128]{1,0:T(8,128)(2,1)S(1)}, bf16[1152,128]{1,0:T(8,128)(2,1)S(1)}, u32[]{:S(2)}, u32[]{:S(2)}) collective-permute-start(bf16[1152,128]{1,0:T(8,128)(2,1)S(1)} %get-tuple-element.35.refs_0_), channel_id=1, source_target_pairs={{0,3},{1,0},{2,1},{3,2},{128,129},{129,130},{130,131},{131,128},{4... | collective-permute-start | bytes 884744 | tf_op jit(solution)/shard_map/ppermute | solution.py:459
  66.9 6.2 %collective-permute-start.9 = (bf16[1152,128]{1,0:T(8,128)(2,1)S(1)}, bf16[1152,128]{1,0:T(8,128)(2,1)S(1)}, u32[]{:S(2)}, u32[]{:S(2)}) collective-permute-start(bf16[1152,128]{1,0:T(8,128)(2,1)S(1)} %get-tuple-element.35.refs_0_), channel_id=1, source_target_pairs={{0,1},{1,2},{2,3},{3,0},{128,131},{129,128},{130,129},{131,130},{4... | collective-permute-start | bytes 884744 | tf_op jit(solution)/shard_map/ppermute | solution.py:459
  68.4 10.9 %collective-permute-start.7 = (bf16[1152,128]{1,0:T(8,128)(2,1)S(1)}, bf16[1152,128]{1,0:T(8,128)(2,1)S(1)}, u32[]{:S(2)}, u32[]{:S(2)}) collective-permute-start(bf16[1152,128]{1,0:T(8,128)(2,1)S(1)} %get-tuple-element.34.refs_0_), channel_id=1, source_target_pairs={{0,1},{1,2},{2,3},{3,0},{128,131},{129,128},{130,129},{131,130},{4... | collective-permute-start | bytes 884744 | tf_op jit(solution)/shard_map/ppermute | solution.py:459
  69.6 9.7 %collective-permute-start.8 = (bf16[1152,128]{1,0:T(8,128)(2,1)S(1)}, bf16[1152,128]{1,0:T(8,128)(2,1)S(1)}, u32[]{:S(2)}, u32[]{:S(2)}) collective-permute-start(bf16[1152,128]{1,0:T(8,128)(2,1)S(1)} %get-tuple-element.34.refs_0_), channel_id=1, source_target_pairs={{0,3},{1,0},{2,1},{3,2},{128,129},{129,130},{130,131},{131,128},{4... | collective-permute-start | bytes 884744 | tf_op jit(solution)/shard_map/ppermute | solution.py:459
  73.1 12.5 %collective-permute-start.11 = (bf16[1152,128]{1,0:T(8,128)(2,1)S(1)}, bf16[1152,128]{1,0:T(8,128)(2,1)S(1)}, u32[]{:S(2)}, u32[]{:S(2)}) collective-permute-start(bf16[1152,128]{1,0:T(8,128)(2,1)S(1)} %collective-permute-done.9.refs_1_), channel_id=1, source_target_pairs={{0,1},{1,2},{2,3},{3,0},{128,131},{129,128},{130,129},{131,130},{4... | collective-permute-start | bytes 884744 | tf_op jit(solution)/shard_map/ppermute | solution.py:459
  79.4 12.8 %collective-permute-start.16 = (bf16[1728,128]{1,0:T(8,128)(2,1)S(1)}, bf16[1728,128]{1,0:T(8,128)(2,1)S(1)}, u32[]{:S(2)}, u32[]{:S(2)}) collective-permute-start(bf16[1728,128]{1,0:T(8,128)(2,1)S(1)} %get-tuple-element.43.refs_0_), channel_id=1, source_target_pairs={{0,1},{1,2},{2,3},{3,0},{128,131},{129,128},{130,129},{131,130},{4... | collective-permute-start | bytes 1327112 | tf_op jit(solution)/shard_map/ppermute | solution.py:459
  82.9 12.3 %collective-permute-start.17 = (bf16[1728,128]{1,0:T(8,128)(2,1)S(1)}, bf16[1728,128]{1,0:T(8,128)(2,1)S(1)}, u32[]{:S(2)}, u32[]{:S(2)}) collective-permute-start(bf16[1728,128]{1,0:T(8,128)(2,1)S(1)} %get-tuple-element.43.refs_0_), channel_id=1, source_target_pairs={{0,3},{1,0},{2,1},{3,2},{128,129},{129,130},{130,131},{131,128},{4... | collective-permute-start | bytes 1327112 | tf_op jit(solution)/shard_map/ppermute | solution.py:459
  82.9 14.9 %collective-permute-start.14 = (bf16[1152,128]{1,0:T(8,128)(2,1)S(1)}, bf16[1152,128]{1,0:T(8,128)(2,1)S(1)}, u32[]{:S(2)}, u32[]{:S(2)}) collective-permute-start(bf16[1152,128]{1,0:T(8,128)(2,1)S(1)} %collective-permute-done.7.refs_1_), channel_id=1, source_target_pairs={{0,1},{1,2},{2,3},{3,0},{128,131},{129,128},{130,129},{131,130},{4... | collective-permute-start | bytes 884744 | tf_op jit(solution)/shard_map/ppermute | solution.py:459
  95.1 14.8 %collective-permute-start.18 = (bf16[1728,128]{1,0:T(8,128)(2,1)S(1)}, bf16[1728,128]{1,0:T(8,128)(2,1)S(1)}, u32[]{:S(2)}, u32[]{:S(2)}) collective-permute-start(bf16[1728,128]{1,0:T(8,128)(2,1)S(1)} %collective-permute-done.16.refs_1_), channel_id=1, source_target_pairs={{0,1},{1,2},{2,3},{3,0},{128,131},{129,128},{130,129},{131,130},{4... | collective-permute-start | bytes 1327112 | tf_op jit(solution)/shard_map/ppermute | solution.py:459
  95.1 11.0 %collective-permute-start.12 = (bf16[1152,128]{1,0:T(8,128)(2,1)S(1)}, bf16[1152,128]{1,0:T(8,128)(2,1)S(1)}, u32[]{:S(2)}, u32[]{:S(2)}) collective-permute-start(bf16[1152,128]{1,0:T(8,128)(2,1)S(1)} %get-tuple-element.37.refs_0_), channel_id=1, source_target_pairs={{0,1},{1,2},{2,3},{3,0},{128,131},{129,128},{130,129},{131,130},{4... | collective-permute-start | bytes 884744 | tf_op jit(solution)/shard_map/ppermute | solution.py:459
  95.2 11.0 %collective-permute-start.13 = (bf16[1152,128]{1,0:T(8,128)(2,1)S(1)}, bf16[1152,128]{1,0:T(8,128)(2,1)S(1)}, u32[]{:S(2)}, u32[]{:S(2)}) collective-permute-start(bf16[1152,128]{1,0:T(8,128)(2,1)S(1)} %get-tuple-element.37.refs_0_), channel_id=1, source_target_pairs={{0,3},{1,0},{2,1},{3,2},{128,129},{129,130},{130,131},{131,128},{4... | collective-permute-start | bytes 884744 | tf_op jit(solution)/shard_map/ppermute | solution.py:459
  106.2 10.4 %collective-permute-start.15 = (bf16[1152,128]{1,0:T(8,128)(2,1)S(1)}, bf16[1152,128]{1,0:T(8,128)(2,1)S(1)}, u32[]{:S(2)}, u32[]{:S(2)}) collective-permute-start(bf16[1152,128]{1,0:T(8,128)(2,1)S(1)} %collective-permute-done.12.refs_1_), channel_id=1, source_target_pairs={{0,1},{1,2},{2,3},{3,0},{128,131},{129,128},{130,129},{131,130},{4... | collective-permute-start | bytes 884744 | tf_op jit(solution)/shard_map/ppermute | solution.py:459
  119.0 12.3 %collective-permute-start.19 = (bf16[8,64,512]{2,1,0:T(8,128)(2,1)}, bf16[8,64,512]{2,1,0:T(8,128)(2,1)S(1)}, u32[]{:S(2)}, u32[]{:S(2)}) collective-permute-start(bf16[8,64,512]{2,1,0:T(8,128)(2,1)} %get-tuple-element.46), channel_id=1, source_target_pairs={{0,128},{128,0},{1,129},{129,1},{2,130},{130,2},{3,131},{131,3},{4... | collective-permute-start | bytes 1572872 | tf_op jit(solution)/shard_map/ppermute | solution.py:575
  123.1 8.1 %collective-permute-start.20 = (bf16[8,4096]{1,0:T(8,128)(2,1)}, bf16[8,4096]{1,0:T(8,128)(2,1)S(1)}, u32[]{:S(2)}, u32[]{:S(2)}) collective-permute-start(bf16[8,4096]{1,0:T(8,128)(2,1)} %get-tuple-element.47), channel_id=1, source_target_pairs={{0,128},{128,0},{1,129},{129,1},{2,130},{130,2},{3,131},{131,3},{4... | collective-permute-start | bytes 196616 | tf_op jit(solution)/shard_map/ppermute | solution.py:575
  (23 other events, 345.9 us)
